TPU v7x, 32 devices: a whole 2x2x4 slice. The times are simulated.
32 devices in a mesh: seq: 16 (over z, y, x), tp: 2 (over core).
Axes of the slice: x: 2, y: 2, z: 4, core: 2. Of those that a mesh axis runs over, the one named last changes fastest.
Arguments:
- queries: bfloat16 [2048, 3072], P('seq', 'tp'), may hold values from -6 to 6
- key_rows: bfloat16 [2048, 3072], P('seq', 'tp'), may hold values from -6 to 6
- value_rows: bfloat16 [2048, 3072], P('seq', 'tp'), may hold values from -6 to 6
- gate_input: bfloat16 [2048, 3072], P('seq', 'tp'), may hold values from -8 to 8
- norm_gain: float32 [3072], replicated, may hold values from 0.1 to 1.9
- doc_ids: int32 [2048], P('seq'), may hold values from 0 to 7, never falling along the last dimension, each value on 1 to 1024 neighbouring positions
- out_weight: bfloat16 [3072, 6144], P(None, 'tp'), may hold values from -0.109375 to 0.109375
Outputs:
- layer_out: bfloat16 [2048, 6144], P('seq', 'tp')
Inputs may be any that keep to these rules, and one draw needn't show every extreme that they name: doc_ids never fall along the stream; every document id is used, each document has 1 to 1024 tokens and one has exactly 1024.
All inputs are finite; a program needn't handle non-finite values.
Results may differ from a plain program's by a relative error of at most 0.015.
Values may be sent and summed in bfloat16 or wider, within the bound.
No kernel may reach another device: no remote copies, remote signals or barrier semaphores. Data moves between devices by JAX's collectives and lax.ppermute only.
A program may use at most 64 MiB of HBM per device.

v0:
```python
import jax
import jax.numpy as jnp
from jax import lax
from jax.sharding import PartitionSpec as P

HEADS = 32
HD = 96


norm_eps = 1e-05


def carried_in(value, axis, combine, identity):
    size, index = (lax.axis_size(axis), lax.axis_index(axis))
    everything = jax.tree.map(
        lambda part, kind: lax.all_gather(part.astype(kind), axis), value, (jnp.bfloat16, jnp.int32)
    )
    start = jax.tree.map(
        lambda part, zero: jnp.broadcast_to(jnp.asarray(zero, part.dtype), part.shape),
        value,
        identity,
    )

    def turn(k, before):
        reached = k < index
        new = combine(
            before, jax.tree.map(lambda part, own: part[k].astype(own.dtype), everything, value)
        )
        return jax.tree.map(lambda a, b: jnp.where(reached, a, b), new, before)

    return lax.fori_loop(0, size, turn, start)


def join_states(earlier, later):
    empty_later = later[1] < 0
    summed = later[0] + jnp.where(earlier[1] == later[1], earlier[0], 0.0)
    state = jnp.where(empty_later, earlier[0], summed)
    last_doc = jnp.where(empty_later, earlier[1], later[1])
    return (state, last_doc)


def on_device(queries, key_rows, value_rows, gate_input, norm_gain, doc_ids, out_weight):
    rows = queries.shape[0]
    local_width = queries.shape[1]
    local_heads = local_width // HD
    width = HEADS * HD
    highest = lax.Precision.HIGHEST
    query3 = queries.reshape(rows, local_heads, HD)
    key3 = key_rows.reshape(rows, local_heads, HD)
    value3 = value_rows.reshape(rows, local_heads, HD)
    last_doc = doc_ids[-1]
    own_keys = jnp.where((doc_ids == last_doc)[:, None, None], key3, jnp.zeros_like(key3))
    own = jnp.einsum("thd,the->hde", own_keys, value3, preferred_element_type=jnp.float32)
    identity = (jnp.zeros_like(own), jnp.array(-1, jnp.int32))
    prefix_state, prefix_doc = carried_in((own, last_doc), "seq", join_states, identity)
    scores = jnp.einsum("thd,shd->hts", query3, key3, preferred_element_type=jnp.float32)
    causal = jnp.arange(rows)[:, None] >= jnp.arange(rows)[None, :]
    keep = causal & (doc_ids[:, None] == doc_ids[None, :])
    scores = jnp.where(keep[None], scores, 0.0)
    value_f = value3.astype(jnp.float32)
    intra = jnp.einsum("hts,shd->thd", scores, value_f, precision=highest)
    carried = jnp.einsum(
        "thd,hde->the", query3.astype(jnp.float32), prefix_state, precision=highest
    )
    attn_full = intra + jnp.where((doc_ids == prefix_doc)[:, None, None], carried, 0.0)
    attn = attn_full.reshape(rows, local_width).astype(jnp.bfloat16)
    values = attn.astype(jnp.float32)
    squares = jnp.sum(values * values, axis=1)
    totals = lax.psum(squares, "tp")
    scale = lax.rsqrt(totals / width + norm_eps)
    offset = lax.axis_index("tp") * local_width
    gain_part = lax.dynamic_slice_in_dim(norm_gain, offset, local_width)
    hidden = (
        values
        * scale[:, None]
        * gain_part[None, :]
        * jax.nn.sigmoid(gate_input.astype(jnp.float32))
    ).astype(jnp.bfloat16)
    result = jnp.dot(
        lax.all_gather(hidden, "tp", axis=1, tiled=True),
        out_weight,
        preferred_element_type=jnp.float32,
    )
    return result.astype(jnp.bfloat16)


def solution(mesh):
    return jax.shard_map(
        on_device,
        mesh=mesh,
        in_specs=(
            P("seq", "tp"),
            P("seq", "tp"),
            P("seq", "tp"),
            P("seq", "tp"),
            P(),
            P("seq"),
            P(None, "tp"),
        ),
        out_specs=P("seq", "tp"),
        check_vma=False,
    )
```

profile of v0, /device:TPU:0, one launch (start us, length us, event | category | flops | bytes accessed | tf_op | source)
XLA Modules:
  0.0 205.7 jit_solution(3832714060788802754)
XLA Ops:
  6.5 0.0 all-gather.3.cloned.1.call-start
  6.5 1.2 dynamic-slice
  7.8 2.0 fusion.9
  9.7 1.3 broadcast_compare_fusion.1
  11.1 1.2 copy.20
  12.3 1.2 copy.21
  13.5 1.1 convolution_convert_fusion.1
  14.7 0.0 all-gather.3.cloned.1.call-update
  14.7 1.2 copy.19
  15.9 0.8 dynamic_slice.17
  16.7 16.3 %all-reduce = s32[16]{0:T(128)S(1)} all-reduce(s32[16]{0:T(128)S(1)} %get-tuple-element.151), channel_id=1, replica_groups=mesh['seq'=16,'tp'=2] {'seq'}, use_global_device_ids=true, to_apply=%add | all-reduce | flops 16 | bytes 128
  33.0 0.8 fusion.7
  33.8 0.4 convolution_select_fusion
  34.2 77.7 %all-gather.3.cloned.1.call-done = bf16[256,96,96]{2,1,0:T(8,128)(2,1)} async-done(((bf16[16,96,96]{2,1,0:T(8,128)(2,1)}), bf16[256,96,96]{2,1,0:T(8,128)(2,1)}) %all-gather.3.cloned.1.call-update) | async-done | bytes 4718608 | tf_op jit(solution)/shard_map/all_gather | solution.py:16
  111.9 68.0 %while.16 = (s32[]{:T(128)}, f32[16,96,96]{2,1,0:T(8,128)S(1)}, s32[]{:T(128)}, s32[]{:T(128)}, s32[16]{0:T(128)S(1)}, /*index=5*/bf16[16,16,96,96]{3,2,1,0:T(8,128)(2,1)}, s32[]{:T(128)}, s32[]{:T(128)}) while((s32[]{:T(128)}, f32[16,96,96]{2,1,0:T(8,128)S(1)}, s32[]{:T(128)}, s32[]{:T(128)}, s32[16]{0:T(128)S(1)}, ...), condition=%wide.region_1.2_spmd.clone, body=%wide.region_0.1_spmd.clone.sunk | while | flops 884744 | bytes 1474727 | solution.py:31
  111.9 0.6 dynamic_slice.24
  113.8 1.7 select_select_fusion.2
  116.1 0.6 dynamic_slice.24
  118.0 1.7 select_select_fusion.2
  120.4 0.6 dynamic_slice.24
  122.3 1.7 select_select_fusion.2
  124.6 0.6 dynamic_slice.24
  126.5 1.7 select_select_fusion.2
  128.9 0.6 dynamic_slice.24
  130.8 1.7 select_select_fusion.2
  133.1 0.6 dynamic_slice.24
  135.0 1.7 select_select_fusion.2
  137.4 0.6 dynamic_slice.24
  139.3 1.7 select_select_fusion.2
  141.6 0.6 dynamic_slice.24
  143.5 1.7 select_select_fusion.2
  145.9 0.6 dynamic_slice.24
  147.8 1.7 select_select_fusion.2
  150.1 0.6 dynamic_slice.24
  152.0 1.7 select_select_fusion.2
  154.4 0.6 dynamic_slice.24
  156.3 1.7 select_select_fusion.2
  158.6 0.6 dynamic_slice.24
  160.5 1.7 select_select_fusion.2
  162.9 0.6 dynamic_slice.24
  164.8 1.7 select_select_fusion.2
  167.1 0.6 dynamic_slice.24
  169.0 1.7 select_select_fusion.2
  171.4 0.6 dynamic_slice.24
  173.3 1.7 select_select_fusion.2
  175.6 0.6 dynamic_slice.24
  177.5 1.7 select_select_fusion.2
  179.9 0.7 broadcast_compare_fusion
  180.5 0.8 fusion.1
  181.3 1.2 multiply_reduce_fusion
  182.6 0.3 copy.23
  182.8 2.5 %psum.7 = f32[128]{0:T(128)S(1)} all-reduce(f32[128]{0:T(128)S(1)} %get-tuple-element.152), channel_id=1, replica_groups=mesh['seq'=16,'tp'=2] {'tp'}, use_global_device_ids=true, to_apply=%region_3.4 | all-reduce | flops 128 | bytes 1024 | tf_op jit(solution)/shard_map/psum | solution.py:69
  185.3 1.2 multiply_convert_fusion
  186.6 2.4 %all_gather.15 = bf16[128,3072]{1,0:T(8,128)(2,1)S(1)} all-gather(bf16[128,1536]{1,0:T(8,128)(2,1)S(1)} %multiply_convert_fusion), channel_id=1, replica_groups=mesh['seq'=16,'tp'=2] {'tp'}, dimensions={1}, use_global_device_ids=true | all-gather | bytes 1179648 | tf_op jit(solution)/shard_map/all_gather | solution.py:80
  188.9 9.9 %convolution_convert_fusion = bf16[128,3072]{1,0:T(8,128)(2,1)} fusion(bf16[128,3072]{1,0:T(8,128)(2,1)S(1)} %all_gather.15, bf16[3072,3072]{1,0:T(8,128)(2,1)} %param.15), kind=kOutput, calls=%fused_computation.2 | convolution fusion | flops 2416312320 | bytes 20447232 | tf_op jit(solution)/shard_map/dot_general | solution.py:79
  (3 shorter events, 0.0 us)
Async XLA Ops:
  6.5 105.3 %all-gather.3.cloned.1.call-start = ((), (), s32[]{:S(2)}) async-start(), calls=%async_computation | async-start | bytes 6684672 | tf_op jit(solution)/shard_map/all_gather | solution.py:16
Sparse Core Ops, SparseCore 0:
  14.8 97.0 all-gather.2
where the time goes:
time: 207 us; the launch traced here: 206 us
  waiting for transfers between devices  77.7 us (38%)
  loops' own time  31.7 us (15%)
  other arithmetic  31 us (15%)
  blocking collectives  21.1 us (10%)
  local copies, waits for them, and re-layouts  17.3 us (8%)
  between operations  13.5 us (7%)
  matrix products  13.4 us (6%)
    all_gather x1, waiting for transfers between devices, carried_in(): lax.all_gather(part.astype(kind), axis)  77.7 us
    another operation x1, loops' own time, carried_in(): return lax.fori_loop(0, size, turn, start)  31.7 us
    select_n x16, other arithmetic, turn(): return jax.tree.map(lambda a, b: jnp.where(reached, a, b), new, before)  26.9 us
    unnamed x1, blocking collectives  16.3 us
    dot_general x1, matrix products, on_device(): jnp.dot(lax.all_gather(hidden, 'tp', axis=1, tiled=True), out_weight, pre...  9.91 us
    dynamic_slice x16, local copies, waits for them, and re-layouts, turn(): part[k].astype(own.dtype)  9.38 us
    unnamed x5, local copies, waits for them, and re-layouts  4.88 us
  transfers between devices with their start and end apart: 1, of which 1 were waited for; matrix products, arithmetic and copies ran while one was open for 2% of the time, Pallas kernels for 0%

commit v1 on v0

v1 whole, which is shorter than its diff:
```python
import functools

import jax
import jax.numpy as jnp
from jax import lax
from jax.experimental import pallas as pl
from jax.experimental.pallas import tpu as pltpu
from jax.sharding import PartitionSpec as P

HEADS = 32
HD = 96
WIDTH = HEADS * HD
DOC_MOST = 1024
UNIT = 4
UC = UNIT * HD
LANES = 128
SPLITS = 1
CUT = HD // SPLITS
BODY = CUT * (UC // LANES)
IDS = 16
PACKET = BODY + IDS
LOADS = 4
norm_eps = 1e-05

bf16 = jnp.bfloat16
f32 = jnp.float32
IN_VMEM = pl.BlockSpec(memory_space=pltpu.VMEM)
IN_HBM = pl.BlockSpec(memory_space=pltpu.HBM)


def call(kernel, outs, args, name, limit=16, scratch=(), far_in=(), far_out=(), flops=0, moved=0):
    args = [
        pltpu.with_memory_space_constraint(arg, pltpu.HBM) if i in far_in else arg
        for i, arg in enumerate(args)
    ]
    return pl.pallas_call(
        kernel,
        out_shape=outs,
        in_specs=[IN_HBM if i in far_in else IN_VMEM for i in range(len(args))],
        out_specs=[IN_HBM if i in far_out else IN_VMEM for i in range(len(outs))],
        scratch_shapes=list(scratch),
        compiler_params=pltpu.CompilerParams(vmem_limit_bytes=limit << 20),
        cost_estimate=pl.CostEstimate(flops=flops, bytes_accessed=moved, transcendentals=0),
        name=name,
    )(*args)


def fetch(pairs, sems):
    copies = [pltpu.make_async_copy(src, dst, sems.at[i]) for i, (src, dst) in enumerate(pairs)]
    for copy in copies:
        copy.start()
    return copies


def lane_head(shape):
    return lax.broadcasted_iota(jnp.int32, shape, 1) // HD


def diagonal(blocks, head):
    total = blocks[0]
    for a in range(1, UNIT):
        total = jnp.where(head == a, blocks[a], total)
    return total


def id_column(ids):
    rows = ids.shape[1]
    return jnp.broadcast_to(ids, (rows, rows)).T


def place_in(group):
    return lax.rem(lax.axis_index("seq"), group)


def rows_of(index, size):
    return pl.ds(pl.multiple_of(index * size, 16), size)


def own_kernel(group, key_hbm, value_hbm, doc_hbm, *refs):
    packets, (key_ref, value_ref, doc_ref, sems) = refs[:group], refs[group:]
    place = place_in(group)
    columns = []
    pairs = [(doc_hbm, doc_ref)]
    for i in range(group // SPLITS):
        unit = (place ^ (i * SPLITS)) // SPLITS
        cols = pl.ds(pl.multiple_of(unit * UC, LANES), UC)
        columns.append(cols)
        pairs += [(key_hbm.at[:, cols], key_ref.at[:, cols])]
        pairs += [(value_hbm.at[:, cols], value_ref.at[:, cols])]
    copies = fetch(pairs, sems)
    copies[0].wait()
    ids = doc_ref[...].astype(f32)
    first = jnp.min(ids, axis=1, keepdims=True)
    last = jnp.max(ids, axis=1, keepdims=True)
    keep = id_column(ids) == last
    keep = jnp.concatenate([keep] * (UC // keep.shape[1]), axis=1)
    head = lane_head((HD, UC))
    marks = jnp.where(
        lax.broadcasted_iota(jnp.int32, (IDS, LANES), 0) < IDS // 2,
        jnp.broadcast_to(last, (IDS, LANES)),
        jnp.broadcast_to(first, (IDS, LANES)),
    ).astype(bf16)
    for i, cols in enumerate(columns):
        copies[2 * i + 1].wait()
        copies[2 * i + 2].wait()
        keys = jnp.where(keep, key_ref[:, cols], jnp.zeros((), bf16))
        full = lax.dot_general(
            keys, value_ref[:, cols], (((0,), (0,)), ((), ())), preferred_element_type=f32
        )
        state = diagonal([full[a * HD : (a + 1) * HD] for a in range(UNIT)], head).astype(bf16)
        for s in range(SPLITS):
            out_ref = packets[i * SPLITS + s]
            part = state[:CUT]
            for r in range(1, SPLITS):
                mine = lax.rem(place ^ s, SPLITS) == r
                part = jnp.where(mine, state[r * CUT : (r + 1) * CUT], part)
            for c in range(UC // LANES):
                out_ref[c * CUT : (c + 1) * CUT] = part[:, c * LANES : (c + 1) * LANES]
            out_ref[BODY:] = marks


def read_packet(ref, base=0):
    marks = ref[base + BODY : base + PACKET].astype(f32)
    return ref[base : base + BODY].astype(f32), marks[0:1], marks[IDS // 2 : IDS // 2 + 1]


def group_kernel(group, beside_ref, *refs):
    packets, out_ref = [read_packet(ref) for ref in refs[:group]], refs[group]
    last = functools.reduce(jnp.maximum, [item[1] for item in packets])
    total = jnp.zeros((BODY, LANES), f32)
    for state, now, _ in packets:
        total = total + jnp.where(now == last, state, 0.0)
    out_ref[:BODY] = total.astype(bf16)
    out_ref[BODY:] = jnp.broadcast_to(last, (IDS, LANES)).astype(bf16)


def prefix_kernel(group, matchings, beside_ref, *refs):
    count = group + len(matchings)
    packets, earlier = refs[:group], refs[group:count]
    outs, (in_order, done) = refs[count:-2], refs[-2:]
    place = place_in(group)
    own_group = lax.axis_index("seq") // group
    for k in range(group):
        in_order[rows_of(place ^ k, PACKET)] = packets[k][...]
    own, last, first = read_packet(in_order)
    before = jnp.zeros((BODY, LANES), f32)
    for ref, (shift, odd) in zip(earlier, matchings):
        valid = jnp.where(lax.rem(own_group // shift, 2) == 1 - odd, 1.0, 0.0)
        state, now, _ = read_packet(ref)
        before = before + jnp.where(now == first, valid, 0.0) * state
    for j in range(group):
        if j:
            before_last = last
            through = own + jnp.where(last == first, before, 0.0)
            own, last, first = read_packet(in_order, j * PACKET)
            before = jnp.where(before_last == first, through, 0.0)
        done[j * BODY : (j + 1) * BODY] = before.astype(bf16)
    for k in range(group):
        outs[k][...] = done[rows_of(place ^ k, BODY)]


def start_load(weight_hbm, third, out_ref, sems):
    rows, columns = out_ref.shape
    step = rows // LOADS
    return fetch(
        [
            (
                weight_hbm.at[pl.ds(i * step, step), pl.ds(third * columns, columns)],
                out_ref.at[pl.ds(i * step, step)],
            )
            for i in range(LOADS)
        ],
        sems,
    )


def load_kernel(third, after_ref, weight_hbm, out_ref, sems):
    for copy in start_load(weight_hbm, third, out_ref, sems):
        copy.wait()


def intra_kernel(
    after_ref, query_hbm, key_hbm, value_hbm, gate_hbm, gain_hbm, doc_hbm, weight_hbm,
    intra_ref, scale_ref, open_ref, weight_ref,
    query_ref, key_ref, value_ref, gate_ref, gain_ref, doc_ref, sems, load_sems,
):
    rows, width = query_ref.shape
    copies = fetch(
        [
            (doc_hbm, doc_ref),
            (query_hbm, query_ref),
            (key_hbm, key_ref),
            (value_hbm, value_ref),
            (gain_hbm, gain_ref),
            (gate_hbm, gate_ref),
        ],
        sems,
    )
    loads = start_load(weight_hbm, 0, weight_ref, load_sems)
    copies[0].wait()
    ids = doc_ref[...].astype(f32)
    column = id_column(ids)
    causal = lax.broadcasted_iota(jnp.int32, (rows, rows), 0) >= lax.broadcasted_iota(
        jnp.int32, (rows, rows), 1
    )
    keep = jnp.concatenate([(column == ids) & causal] * UNIT, axis=0)
    opened = column == jnp.min(ids, axis=1, keepdims=True)
    opened = jnp.concatenate([opened] * (UC // rows), axis=1)
    head = lane_head((rows, UC))
    part = lax.axis_index("tp")
    for copy in copies[1:4]:
        copy.wait()
    for u in range(width // UC):
        cols = slice(u * UC, (u + 1) * UC)
        query = query_ref[:, cols]
        open_ref[:, cols] = jnp.where(opened, query, jnp.zeros((), bf16))
        stacked = jnp.concatenate(
            [jnp.where(head == a, query, jnp.zeros((), bf16)) for a in range(UNIT)], axis=0
        )
        scores = lax.dot_general(
            stacked, key_ref[:, cols], (((1,), (1,)), ((), ())), preferred_element_type=f32
        )
        scores = jnp.where(keep, scores, 0.0).astype(bf16)
        mixed = jnp.dot(scores, value_ref[:, cols], preferred_element_type=f32)
        intra_ref[:, cols] = diagonal(
            [mixed[a * rows : (a + 1) * rows] for a in range(UNIT)], head
        )
    copies[4].wait()
    copies[5].wait()
    for u in range(width // UC):
        cols = slice(u * UC, (u + 1) * UC)
        gain = gain_ref[:, pl.ds(pl.multiple_of(part * width + u * UC, LANES), UC)]
        scale_ref[:, cols] = gain * jax.nn.sigmoid(gate_ref[:, cols].astype(f32))
    for load in loads:
        load.wait()


def hidden_kernel(group, open_ref, intra_ref, scale_ref, beside_ref, *refs):
    states, (out_ref, in_order) = refs[:group], refs[group:]
    rows, width = open_ref.shape
    place = place_in(group)
    for k in range(group):
        in_order[rows_of(place ^ k, BODY)] = states[k][...]
    head = lane_head((HD, UC))
    squares = jnp.zeros((rows, LANES), f32)
    for u in range(width // UC):
        cols = slice(u * UC, (u + 1) * UC)
        pieces = []
        for s in range(SPLITS):
            base = (u * SPLITS + s) * BODY
            pieces.append(
                jnp.concatenate(
                    [
                        in_order[base + c * CUT : base + (c + 1) * CUT]
                        for c in range(UC // LANES)
                    ],
                    axis=1,
                )
            )
        state = jnp.concatenate(pieces, axis=0)
        spread = jnp.concatenate(
            [jnp.where(head == a, state, jnp.zeros((), bf16)) for a in range(UNIT)], axis=0
        )
        carried = jnp.dot(open_ref[:, cols], spread, preferred_element_type=f32)
        attn = (intra_ref[:, cols] + carried).astype(bf16).astype(f32)
        power = attn * attn
        for c in range(UC // LANES):
            squares = squares + power[:, c * LANES : (c + 1) * LANES]
        out_ref[:, cols] = (attn * scale_ref[:, cols]).astype(bf16)
    total = jnp.broadcast_to(jnp.sum(squares, axis=1, keepdims=True), (rows, LANES))
    high = total.astype(bf16)
    out_ref[:, width : width + LANES] = high
    out_ref[:, width + LANES :] = (total - high.astype(f32)).astype(bf16)


def near_kernel(hidden_ref, *refs):
    *weights, out_ref = refs
    depth = hidden_ref.shape[1] - 2 * LANES
    rows = pl.ds(pl.multiple_of(lax.axis_index("tp") * depth, LANES), depth)
    wide = weights[0].shape[1]
    for i, weight in enumerate(weights):
        out_ref[:, i * wide : (i + 1) * wide] = jnp.dot(
            hidden_ref[:, :depth], weight[rows], preferred_element_type=f32
        )


def far_kernel(parts, near_ref, *refs):
    weights, hidden, (out_hbm, out_ref, sems) = refs[:3], refs[3:-3], refs[-3:]
    depth = hidden[0].shape[1] - 2 * LANES
    wide = weights[0].shape[1]
    me = lax.axis_index("tp")
    total = None
    for ref in hidden:
        one = ref[:, depth : depth + LANES].astype(f32) + ref[:, depth + LANES :].astype(f32)
        total = one if total is None else total + one
    norm = lax.rsqrt(total / WIDTH + norm_eps)
    norm = jnp.concatenate([norm] * (wide // LANES), axis=1)
    copies = []
    for i, weight in enumerate(weights):
        cols = pl.ds(i * wide, wide)
        value = near_ref[:, cols]
        for k in range(1, parts):
            owner = lax.rem(me + parts - k, parts)
            rows = pl.ds(pl.multiple_of(owner * depth, LANES), depth)
            value = value + jnp.dot(
                hidden[k][:, :depth], weight[rows], preferred_element_type=f32
            )
        out_ref[:, cols] = (value * norm).astype(bf16)
        copy = pltpu.make_async_copy(out_ref.at[:, cols], out_hbm.at[:, cols], sems.at[i])
        copy.start()
        copies.append(copy)
    for copy in copies:
        copy.wait()


def on_device(queries, key_rows, value_rows, gate_input, norm_gain, doc_ids, out_weight):
    rows, width = queries.shape
    features = out_weight.shape[1]
    blocks, parts = lax.axis_size("seq"), lax.axis_size("tp")
    units = width // UC
    group = units * SPLITS
    back = -(-(-(-(DOC_MOST - 1) // rows)) // group)
    matchings = [(s, odd) for s in range(1, back + 1) for odd in range(2) if (odd + 1) * s * group < blocks]
    ids = doc_ids.reshape(1, rows)
    gain = norm_gain.reshape(1, WIDTH)
    dma = pltpu.SemaphoreType.DMA
    block16 = pltpu.VMEM((rows, width), bf16)
    ids_block = pltpu.VMEM((1, rows), jnp.int32)
    packet = jax.ShapeDtypeStruct((PACKET, LANES), bf16)
    body = jax.ShapeDtypeStruct((BODY, LANES), bf16)
    wide = jax.ShapeDtypeStruct((rows, width), f32)
    third = pltpu.VMEM((out_weight.shape[0], features // 3), bf16)

    def swap(value, pairs):
        return lax.ppermute(value, "seq", pairs)

    def trade(values):
        return [values[0]] + [
            swap(values[k], [(i, i ^ k) for i in range(blocks)]) for k in range(1, group)
        ]

    def matching(shift, odd):
        step = shift * group
        lower = [i for i in range(blocks - step) if (i // step) % 2 == odd]
        return [(i, i + step) for i in lower] + [(i + step, i) for i in lower]

    def load(index, after):
        return call(
            functools.partial(load_kernel, index),
            [third],
            (after, out_weight),
            "weight_load",
            scratch=[dma((LOADS,))],
            far_in=(1,),
            moved=2 * out_weight.size * 2 // 3,
        )[0]

    own = call(
        functools.partial(own_kernel, group),
        [packet] * group,
        (key_rows, value_rows, ids),
        "own_states",
        scratch=[block16, block16, ids_block, dma((1 + 2 * units,))],
        far_in=(0, 1, 2),
    )
    packets = trade(own)
    intra, scale, opened, weight0 = call(
        intra_kernel,
        [wide, wide, jax.ShapeDtypeStruct((rows, width), bf16), third],
        (own[0], queries, key_rows, value_rows, gate_input, gain, ids, out_weight),
        "intra",
        scratch=[block16] * 4 + [pltpu.VMEM((1, WIDTH), f32), ids_block, dma((6,)), dma((LOADS,))],
        far_in=range(1, 8),
        flops=4 * rows * rows * UNIT * width,
        moved=2 * out_weight.size * 2 // 3,
    )
    (summed,) = call(
        functools.partial(group_kernel, group), [packet], (intra, *packets), "group_state"
    )
    earlier = [swap(summed, matching(s, odd)) for s, odd in matchings]
    weight1 = load(1, summed)
    prefixes = call(
        functools.partial(prefix_kernel, group, matchings),
        [body] * group,
        (weight1, *packets, *earlier),
        "prefix_states",
        scratch=[pltpu.VMEM((group * PACKET, LANES), bf16), pltpu.VMEM((group * BODY, LANES), bf16)],
    )
    states = trade(prefixes)
    weight2 = load(2, prefixes[0])
    (hidden,) = call(
        functools.partial(hidden_kernel, group),
        [jax.ShapeDtypeStruct((rows, width + 2 * LANES), bf16)],
        (opened, intra, scale, weight2, *states),
        "hidden",
        scratch=[pltpu.VMEM((group * BODY, LANES), bf16)],
    )
    others = [
        lax.ppermute(hidden, "tp", [(i, (i + k) % parts) for i in range(parts)])
        for k in range(1, parts)
    ]
    weights = (weight0, weight1, weight2)
    (near,) = call(
        near_kernel,
        [jax.ShapeDtypeStruct((rows, features), f32)],
        (hidden, *weights),
        "near",
        flops=2 * rows * width * features,
        moved=2 * width * features,
    )
    (out,) = call(
        functools.partial(far_kernel, parts),
        [jax.ShapeDtypeStruct((rows, features), bf16)],
        (near, *weights, hidden, *others),
        "far",
        scratch=[pltpu.VMEM((rows, features), bf16), dma((3,))],
        far_out=(0,),
        flops=2 * rows * width * features,
        moved=2 * width * features,
    )
    return out


def solution(mesh):
    return jax.shard_map(
        on_device,
        mesh=mesh,
        in_specs=(
            P("seq", "tp"),
            P("seq", "tp"),
            P("seq", "tp"),
            P("seq", "tp"),
            P(),
            P("seq"),
            P(None, "tp"),
        ),
        out_specs=P("seq", "tp"),
        check_vma=False,
    )
```

time: 207 us -> 33.2 us (0.16)
  waiting for transfers between devices: 77.7 us -> 2.75 us
  loops' own time: 31.7 us -> 0 us
  other arithmetic: 31 us -> 0 us
  blocking collectives: 21.1 us -> 0 us
  local copies, waits for them, and re-layouts: 17.3 us -> 0 us
  Pallas kernels: 0 us -> 15.8 us
  starting transfers between devices: 0.01 us -> 14.4 us
  matrix products: 13.4 us -> 0 us
  between operations: 13.5 us -> 0.13 us
    all_gather x1 -> x0, waiting for transfers between devices: 77.7 us -> none  [carried_in(): lax.all_gather(part.astype(kind), axis)]
    another operation x1 -> x0, loops' own time: 31.7 us -> none  [carried_in(): return lax.fori_loop(0, size, turn, start)]
    select_n x16 -> x0, other arithmetic: 26.9 us -> none  [turn(): return jax.tree.map(lambda a, b: jnp.where(reached, a, b), new, before)]
    unnamed x1 -> x0, blocking collectives: 16.3 us -> none
    pallas_call x0 -> x9, Pallas kernels: none -> 15.8 us  [call(): pl.pallas_call(kernel, out_shape=outs, in_specs=[IN_HBM if i in far_in el...]
    ppermute x0 -> x10, starting transfers between devices: none -> 14.4 us  [the longest x9 14.3 us: swap(): return lax.ppermute(value, 'seq', pairs)]
    dot_general x5 -> x0, matrix products: 13.4 us -> none  [the longest x1 9.91 us: on_device(): jnp.dot(lax.all_gather(hidden, 'tp', axis=1, tiled=True), out_weight, pre...]
    dynamic_slice x17 -> x0, local copies, waits for them, and re-layouts: 10.2 us -> none  [the longest x16 9.38 us: turn(): part[k].astype(own.dtype)]
  transfers between devices with their start and end apart: 1 -> 10, of which waited for: 1 -> 4; matrix products, arithmetic and copies ran while one was open for 2% -> 0% of each run, Pallas kernels for 0% -> 32%
where the time goes in v1:
time: 33.2 us; the launch traced here: 33 us
  Pallas kernels  15.8 us (48%)
  starting transfers between devices  14.4 us (43%)
  waiting for transfers between devices  2.75 us (8%)
    pallas_call x9, Pallas kernels, call(): pl.pallas_call(kernel, out_shape=outs, in_specs=[IN_HBM if i in far_in el...  15.8 us
    ppermute x9, starting transfers between devices, swap(): return lax.ppermute(value, 'seq', pairs)  14.3 us
    ppermute x9, waiting for transfers between devices, swap(): return lax.ppermute(value, 'seq', pairs)  2.36 us
  transfers between devices with their start and end apart: 10, of which 4 were waited for; matrix products, arithmetic and copies ran while one was open for 0% of the time, Pallas kernels for 32%

profile of v1, /device:TPU:0, one launch (start us, length us, event | category | flops | bytes accessed | tf_op | source)
XLA Modules:
  0.0 33.0 jit_solution(14435318323807715488)
XLA Ops:
  0.0 2.2 %own_states.1 = (bf16[304,128]{1,0:T(8,128)(2,1)S(1)}, bf16[304,128]{1,0:T(8,128)(2,1)S(1)}, bf16[304,128]{1,0:T(8,128)(2,1)S(1)}, bf16[304,128]{1,0:T(8,128)(2,1)S(1)}) custom-call(bf16[128,1536]{1,0:T(8,128)(2,1)} %key_hbm.3, bf16[128,1536]{1,0:T(8,128)(2,1)} %value_hbm.3, s32[1,128]{1,0:T(1,128)} %bitcast.3), custom_call_target="tpu_custom_call" | custom-call | tf_op jit(solution)/shard_map/own_states/pallas_call | solution.py:36
  2.2 3.0 %collective-permute-start = (bf16[304,128]{1,0:T(8,128)(2,1)S(1)}, bf16[304,128]{1,0:T(8,128)(2,1)S(1)}, u32[]{:S(2)}, u32[]{:S(2)}) collective-permute-start(bf16[304,128]{1,0:T(8,128)(2,1)S(1)} %get-tuple-element.21), channel_id=1, source_target_pairs={{0,2},{2,0},{4,6},{6,4},{8,10},{10,8},{12,14},{14,12},{16,18},{18,... | collective-permute-start | bytes 233480 | tf_op jit(solution)/shard_map/ppermute | solution.py:335
  5.2 1.5 %collective-permute-start.1 = (bf16[304,128]{1,0:T(8,128)(2,1)S(1)}, bf16[304,128]{1,0:T(8,128)(2,1)S(1)}, u32[]{:S(2)}, u32[]{:S(2)}) collective-permute-start(bf16[304,128]{1,0:T(8,128)(2,1)S(1)} %get-tuple-element.22), channel_id=1, source_target_pairs={{0,4},{2,6},{4,0},{6,2},{8,12},{10,14},{12,8},{14,10},{16,20},{18,... | collective-permute-start | bytes 233480 | tf_op jit(solution)/shard_map/ppermute | solution.py:335
  6.7 0.0 collective-permute-start.2
  6.8 3.4 %intra.1 = (f32[128,1536]{1,0:T(8,128)S(1)}, f32[128,1536]{1,0:T(8,128)S(1)}, bf16[128,1536]{1,0:T(8,128)(2,1)S(1)}, bf16[3072,1024]{1,0:T(8,128)(2,1)S(1)}) custom-call(bf16[304,128]{1,0:T(8,128)(2,1)S(1)} %get-tuple-element.17.after_ref.refs_0_, bf16[128,1536]{1,0:T(8,128)(2,1)} %query_hbm.1, bf16[128,1536]{1,0:T(8,128)(2,1)} %key_hbm.3, ...), custom_call_target="tpu_custom_call" | custom-call | flops 402653184 | bytes 12582912 | tf_op jit(solution)/shard_map/intra/pallas_call | solution.py:36
  10.2 0.0 collective-permute-done.refs_1_
  10.2 0.2 collective-permute-done.1.refs_2_
  10.4 1.6 %collective-permute-done.2.refs_3_ = bf16[304,128]{1,0:T(8,128)(2,1)S(1)} collective-permute-done((bf16[304,128]{1,0:T(8,128)(2,1)S(1)}, bf16[304,128]{1,0:T(8,128)(2,1)S(1)}, u32[]{:S(2)}, u32[]{:S(2)}) %collective-permute-start.2) | collective-permute-done | bytes 77856 | tf_op jit(solution)/shard_map/ppermute | solution.py:335
  12.0 0.1 group_state.1.after_ref
  12.1 2.7 %collective-permute-start.5 = (bf16[304,128]{1,0:T(8,128)(2,1)S(1)}, bf16[304,128]{1,0:T(8,128)(2,1)S(1)}, u32[]{:S(2)}, u32[]{:S(2)}) collective-permute-start(bf16[304,128]{1,0:T(8,128)(2,1)S(1)} %group_state.1.after_ref), channel_id=1, source_target_pairs={{0,16},{2,18},{4,20},{6,22},{8,24},{10,26},{12,28},{14,30},{16,0},... | collective-permute-start | bytes 233480 | tf_op jit(solution)/shard_map/ppermute | solution.py:335
  14.7 0.7 %collective-permute-start.4 = (bf16[304,128]{1,0:T(8,128)(2,1)S(1)}, bf16[304,128]{1,0:T(8,128)(2,1)S(1)}, u32[]{:S(2)}, u32[]{:S(2)}) collective-permute-start(bf16[304,128]{1,0:T(8,128)(2,1)S(1)} %group_state.1.after_ref), channel_id=1, source_target_pairs={{8,16},{10,18},{12,20},{14,22},{16,8},{18,10},{20,12},{22,14},{9,1... | collective-permute-start | bytes 233480 | tf_op jit(solution)/shard_map/ppermute | solution.py:335
  15.4 2.9 %collective-permute-start.3 = (bf16[304,128]{1,0:T(8,128)(2,1)S(1)}, bf16[304,128]{1,0:T(8,128)(2,1)S(1)}, u32[]{:S(2)}, u32[]{:S(2)}) collective-permute-start(bf16[304,128]{1,0:T(8,128)(2,1)S(1)} %group_state.1.after_ref), channel_id=1, source_target_pairs={{0,8},{2,10},{4,12},{6,14},{16,24},{18,26},{20,28},{22,30},{8,0},{... | collective-permute-start | bytes 233480 | tf_op jit(solution)/shard_map/ppermute | solution.py:335
  18.3 2.9 %weight_load.2.beside_ref.refs_1_ = bf16[3072,1024]{1,0:T(8,128)(2,1)S(1)} custom-call(bf16[304,128]{1,0:T(8,128)(2,1)S(1)} %group_state.1.after_ref, bf16[3072,3072]{1,0:T(8,128)(2,1)} %weight_hbm.5), custom_call_target="tpu_custom_call" | custom-call | bytes 12582912 | tf_op jit(solution)/shard_map/weight_load/pallas_call | solution.py:36
  21.2 0.0 collective-permute-done.5.refs_6_
  21.2 0.0 collective-permute-done.4.refs_5_
  21.2 0.0 collective-permute-done.3.refs_4_
  21.2 0.2 prefix_states.1
  21.4 0.6 %collective-permute-start.6 = (bf16[288,128]{1,0:T(8,128)(2,1)S(1)}, bf16[288,128]{1,0:T(8,128)(2,1)S(1)}, u32[]{:S(2)}, u32[]{:S(2)}) collective-permute-start(bf16[288,128]{1,0:T(8,128)(2,1)S(1)} %get-tuple-element.25), channel_id=1, source_target_pairs={{0,2},{2,0},{4,6},{6,4},{8,10},{10,8},{12,14},{14,12},{16,18},{18,... | collective-permute-start | bytes 221192 | tf_op jit(solution)/shard_map/ppermute | solution.py:335
  22.0 1.1 %collective-permute-start.7 = (bf16[288,128]{1,0:T(8,128)(2,1)S(1)}, bf16[288,128]{1,0:T(8,128)(2,1)S(1)}, u32[]{:S(2)}, u32[]{:S(2)}) collective-permute-start(bf16[288,128]{1,0:T(8,128)(2,1)S(1)} %get-tuple-element.26), channel_id=1, source_target_pairs={{0,4},{2,6},{4,0},{6,2},{8,12},{10,14},{12,8},{14,10},{16,20},{18,... | collective-permute-start | bytes 221192 | tf_op jit(solution)/shard_map/ppermute | solution.py:335
  23.2 1.8 %collective-permute-start.8 = (bf16[288,128]{1,0:T(8,128)(2,1)S(1)}, bf16[288,128]{1,0:T(8,128)(2,1)S(1)}, u32[]{:S(2)}, u32[]{:S(2)}) collective-permute-start(bf16[288,128]{1,0:T(8,128)(2,1)S(1)} %get-tuple-element.27), channel_id=1, source_target_pairs={{0,6},{2,4},{4,2},{6,0},{8,14},{10,12},{12,10},{14,8},{16,22},{18,... | collective-permute-start | bytes 221192 | tf_op jit(solution)/shard_map/ppermute | solution.py:335
  25.0 2.9 %weight_load.3.beside_ref.refs_2_ = bf16[3072,1024]{1,0:T(8,128)(2,1)S(1)} custom-call(bf16[288,128]{1,0:T(8,128)(2,1)S(1)} %get-tuple-element.24.after_ref.refs_0_, bf16[3072,3072]{1,0:T(8,128)(2,1)} %weight_hbm.5), custom_call_target="tpu_custom_call" | custom-call | bytes 12582912 | tf_op jit(solution)/shard_map/weight_load/pallas_call | solution.py:36
  27.9 0.0 collective-permute-done.6.refs_1_
  27.9 0.0 collective-permute-done.7.refs_2_
  27.9 0.5 %collective-permute-done.8.refs_3_ = bf16[288,128]{1,0:T(8,128)(2,1)S(1)} collective-permute-done((bf16[288,128]{1,0:T(8,128)(2,1)S(1)}, bf16[288,128]{1,0:T(8,128)(2,1)S(1)}, u32[]{:S(2)}, u32[]{:S(2)}) %collective-permute-start.8) | collective-permute-done | bytes 73760 | tf_op jit(solution)/shard_map/ppermute | solution.py:335
  28.4 0.6 %hidden.1.hidden_ref.refs_3_ = bf16[128,1792]{1,0:T(8,128)(2,1)S(1)} custom-call(bf16[128,1536]{1,0:T(8,128)(2,1)S(1)} %get-tuple-element.18.open_ref, f32[128,1536]{1,0:T(8,128)S(1)} %get-tuple-element.19.beside_ref.intra_ref, f32[128,1536]{1,0:T(8,128)S(1)} %get-tuple-element.20.scale_ref, bf16[3072,1024]{1,0:T(8,128)(2,1)S(1)} %weight_load.3.beside_ref.refs_2_, ...), custom_call_target="tpu_custom_call" | custom-call | tf_op jit(solution)/shard_map/hidden/pallas_call | solution.py:36
  29.0 0.1 collective-permute-start.9
  29.1 1.4 %near.1.near_ref = f32[128,3072]{1,0:T(8,128)S(1)} custom-call(bf16[128,1792]{1,0:T(8,128)(2,1)S(1)} %hidden.1.hidden_ref.refs_3_, bf16[3072,1024]{1,0:T(8,128)(2,1)S(1)} %get-tuple-element.28.refs_0_, bf16[3072,1024]{1,0:T(8,128)(2,1)S(1)} %weight_load.2.beside_ref.refs_1_, bf16[3072,1024]{1,0:T(8,128)(2,1)S(1)} %weight_load.3.beside_ref.refs_2_), custom_call_target="tpu_custom_call" | custom-call | flops 1207959552 | bytes 9437184 | tf_op jit(solution)/shard_map/near/pallas_call | solution.py:36
  30.5 0.4 %collective-permute-done.9.refs_4_ = bf16[128,1792]{1,0:T(8,128)(2,1)S(1)} collective-permute-done((bf16[128,1792]{1,0:T(8,128)(2,1)S(1)}, bf16[128,1792]{1,0:T(8,128)(2,1)S(1)}, u32[]{:S(2)}, u32[]{:S(2)}) %collective-permute-start.9) | collective-permute-done | bytes 458784 | tf_op jit(solution)/shard_map/ppermute | solution.py:399
  30.9 2.2 %far.1 = bf16[128,3072]{1,0:T(8,128)(2,1)} custom-call(f32[128,3072]{1,0:T(8,128)S(1)} %near.1.near_ref, bf16[3072,1024]{1,0:T(8,128)(2,1)S(1)} %get-tuple-element.28.refs_0_, bf16[3072,1024]{1,0:T(8,128)(2,1)S(1)} %weight_load.2.beside_ref.refs_1_, bf16[3072,1024]{1,0:T(8,128)(2,1)S(1)} %weight_load.3.beside_ref.refs_2_, ...), custom_call_target="tpu_custom_call" | custom-call | flops 1207959552 | bytes 9437184 | tf_op jit(solution)/shard_map/far/pallas_call | solution.py:36
Async XLA Ops:
  2.2 8.0 %collective-permute-start = (bf16[304,128]{1,0:T(8,128)(2,1)S(1)}, bf16[304,128]{1,0:T(8,128)(2,1)S(1)}, u32[]{:S(2)}, u32[]{:S(2)}) collective-permute-start(bf16[304,128]{1,0:T(8,128)(2,1)S(1)} %get-tuple-element.21), channel_id=1, source_target_pairs={{0,2},{2,0},{4,6},{6,4},{8,10},{10,8},{12,14},{14,12},{16,18},{18,... | collective-permute-start | bytes 233480 | tf_op jit(solution)/shard_map/ppermute | solution.py:335
  5.2 5.2 %collective-permute-start.1 = (bf16[304,128]{1,0:T(8,128)(2,1)S(1)}, bf16[304,128]{1,0:T(8,128)(2,1)S(1)}, u32[]{:S(2)}, u32[]{:S(2)}) collective-permute-start(bf16[304,128]{1,0:T(8,128)(2,1)S(1)} %get-tuple-element.22), channel_id=1, source_target_pairs={{0,4},{2,6},{4,0},{6,2},{8,12},{10,14},{12,8},{14,10},{16,20},{18,... | collective-permute-start | bytes 233480 | tf_op jit(solution)/shard_map/ppermute | solution.py:335
  6.7 5.3 %collective-permute-start.2 = (bf16[304,128]{1,0:T(8,128)(2,1)S(1)}, bf16[304,128]{1,0:T(8,128)(2,1)S(1)}, u32[]{:S(2)}, u32[]{:S(2)}) collective-permute-start(bf16[304,128]{1,0:T(8,128)(2,1)S(1)} %get-tuple-element.23), channel_id=1, source_target_pairs={{0,6},{2,4},{4,2},{6,0},{8,14},{10,12},{12,10},{14,8},{16,22},{18,... | collective-permute-start | bytes 233480 | tf_op jit(solution)/shard_map/ppermute | solution.py:335
  12.1 9.1 %collective-permute-start.5 = (bf16[304,128]{1,0:T(8,128)(2,1)S(1)}, bf16[304,128]{1,0:T(8,128)(2,1)S(1)}, u32[]{:S(2)}, u32[]{:S(2)}) collective-permute-start(bf16[304,128]{1,0:T(8,128)(2,1)S(1)} %group_state.1.after_ref), channel_id=1, source_target_pairs={{0,16},{2,18},{4,20},{6,22},{8,24},{10,26},{12,28},{14,30},{16,0},... | collective-permute-start | bytes 233480 | tf_op jit(solution)/shard_map/ppermute | solution.py:335
  14.7 6.5 %collective-permute-start.4 = (bf16[304,128]{1,0:T(8,128)(2,1)S(1)}, bf16[304,128]{1,0:T(8,128)(2,1)S(1)}, u32[]{:S(2)}, u32[]{:S(2)}) collective-permute-start(bf16[304,128]{1,0:T(8,128)(2,1)S(1)} %group_state.1.after_ref), channel_id=1, source_target_pairs={{8,16},{10,18},{12,20},{14,22},{16,8},{18,10},{20,12},{22,14},{9,1... | collective-permute-start | bytes 233480 | tf_op jit(solution)/shard_map/ppermute | solution.py:335
  15.4 5.8 %collective-permute-start.3 = (bf16[304,128]{1,0:T(8,128)(2,1)S(1)}, bf16[304,128]{1,0:T(8,128)(2,1)S(1)}, u32[]{:S(2)}, u32[]{:S(2)}) collective-permute-start(bf16[304,128]{1,0:T(8,128)(2,1)S(1)} %group_state.1.after_ref), channel_id=1, source_target_pairs={{0,8},{2,10},{4,12},{6,14},{16,24},{18,26},{20,28},{22,30},{8,0},{... | collective-permute-start | bytes 233480 | tf_op jit(solution)/shard_map/ppermute | solution.py:335
  21.4 6.4 %collective-permute-start.6 = (bf16[288,128]{1,0:T(8,128)(2,1)S(1)}, bf16[288,128]{1,0:T(8,128)(2,1)S(1)}, u32[]{:S(2)}, u32[]{:S(2)}) collective-permute-start(bf16[288,128]{1,0:T(8,128)(2,1)S(1)} %get-tuple-element.25), channel_id=1, source_target_pairs={{0,2},{2,0},{4,6},{6,4},{8,10},{10,8},{12,14},{14,12},{16,18},{18,... | collective-permute-start | bytes 221192 | tf_op jit(solution)/shard_map/ppermute | solution.py:335
  22.0 5.9 %collective-permute-start.7 = (bf16[288,128]{1,0:T(8,128)(2,1)S(1)}, bf16[288,128]{1,0:T(8,128)(2,1)S(1)}, u32[]{:S(2)}, u32[]{:S(2)}) collective-permute-start(bf16[288,128]{1,0:T(8,128)(2,1)S(1)} %get-tuple-element.26), channel_id=1, source_target_pairs={{0,4},{2,6},{4,0},{6,2},{8,12},{10,14},{12,8},{14,10},{16,20},{18,... | collective-permute-start | bytes 221192 | tf_op jit(solution)/shard_map/ppermute | solution.py:335
  23.2 5.3 %collective-permute-start.8 = (bf16[288,128]{1,0:T(8,128)(2,1)S(1)}, bf16[288,128]{1,0:T(8,128)(2,1)S(1)}, u32[]{:S(2)}, u32[]{:S(2)}) collective-permute-start(bf16[288,128]{1,0:T(8,128)(2,1)S(1)} %get-tuple-element.27), channel_id=1, source_target_pairs={{0,6},{2,4},{4,2},{6,0},{8,14},{10,12},{12,10},{14,8},{16,22},{18,... | collective-permute-start | bytes 221192 | tf_op jit(solution)/shard_map/ppermute | solution.py:335
  29.0 1.9 %collective-permute-start.9 = (bf16[128,1792]{1,0:T(8,128)(2,1)S(1)}, bf16[128,1792]{1,0:T(8,128)(2,1)S(1)}, u32[]{:S(2)}, u32[]{:S(2)}) collective-permute-start(bf16[128,1792]{1,0:T(8,128)(2,1)S(1)} %hidden.1.hidden_ref.refs_3_), channel_id=1, source_target_pairs={{0,1},{1,0},{2,3},{3,2},{4,5},{5,4},{6,7},{7,6},{8,9},{9,8},{10,11... | collective-permute-start | bytes 1376264 | tf_op jit(solution)/shard_map/ppermute | solution.py:399

commit v2 on v1

--- a/solution.py
+++ b/solution.py
@@ -14,9 +14,7 @@
 UNIT = 4
 UC = UNIT * HD
 LANES = 128
-SPLITS = 1
-CUT = HD // SPLITS
-BODY = CUT * (UC // LANES)
+BODY = HD * (UC // LANES)
 IDS = 16
 PACKET = BODY + IDS
 LOADS = 4
@@ -68,8 +66,16 @@
     return jnp.broadcast_to(ids, (rows, rows)).T
 
 
-def place_in(group):
-    return lax.rem(lax.axis_index("seq"), group)
+def orders(group):
+    near = sorted(range(group), key=lambda k: (k > 0, -k.bit_count(), k))
+    far = sorted(range(group), key=lambda k: (k > 0, -k.bit_count(), -k))
+    return near, far
+
+
+def helpers(group):
+    place = lax.rem(lax.axis_index("seq"), group)
+    even = lax.rem(lax.axis_index("tp"), 2) == 0
+    return place, [place ^ jnp.where(even, a, b) for a, b in zip(*orders(group))]
 
 
 def rows_of(index, size):
@@ -78,11 +84,9 @@
 
 def own_kernel(group, key_hbm, value_hbm, doc_hbm, *refs):
     packets, (key_ref, value_ref, doc_ref, sems) = refs[:group], refs[group:]
-    place = place_in(group)
     columns = []
     pairs = [(doc_hbm, doc_ref)]
-    for i in range(group // SPLITS):
-        unit = (place ^ (i * SPLITS)) // SPLITS
+    for unit in helpers(group)[1]:
         cols = pl.ds(pl.multiple_of(unit * UC, LANES), UC)
         columns.append(cols)
         pairs += [(key_hbm.at[:, cols], key_ref.at[:, cols])]
@@ -108,15 +112,9 @@
             keys, value_ref[:, cols], (((0,), (0,)), ((), ())), preferred_element_type=f32
         )
         state = diagonal([full[a * HD : (a + 1) * HD] for a in range(UNIT)], head).astype(bf16)
-        for s in range(SPLITS):
-            out_ref = packets[i * SPLITS + s]
-            part = state[:CUT]
-            for r in range(1, SPLITS):
-                mine = lax.rem(place ^ s, SPLITS) == r
-                part = jnp.where(mine, state[r * CUT : (r + 1) * CUT], part)
-            for c in range(UC // LANES):
-                out_ref[c * CUT : (c + 1) * CUT] = part[:, c * LANES : (c + 1) * LANES]
-            out_ref[BODY:] = marks
+        for c in range(UC // LANES):
+            packets[i][c * HD : (c + 1) * HD] = state[:, c * LANES : (c + 1) * LANES]
+        packets[i][BODY:] = marks
 
 
 def read_packet(ref, base=0):
@@ -138,14 +136,15 @@
     count = group + len(matchings)
     packets, earlier = refs[:group], refs[group:count]
     outs, (in_order, done) = refs[count:-2], refs[-2:]
-    place = place_in(group)
+    places = helpers(group)[1]
     own_group = lax.axis_index("seq") // group
-    for k in range(group):
-        in_order[rows_of(place ^ k, PACKET)] = packets[k][...]
+    for place, packet in zip(places, packets):
+        in_order[rows_of(place, PACKET)] = packet[...]
     own, last, first = read_packet(in_order)
     before = jnp.zeros((BODY, LANES), f32)
     for ref, (shift, odd) in zip(earlier, matchings):
-        valid = jnp.where(lax.rem(own_group // shift, 2) == 1 - odd, 1.0, 0.0)
+        second = lax.rem(own_group // shift, 2) == 1 - odd
+        valid = jnp.where(second & (own_group >= shift), 1.0, 0.0)
         state, now, _ = read_packet(ref)
         before = before + jnp.where(now == first, valid, 0.0) * state
     for j in range(group):
@@ -155,8 +154,8 @@
             own, last, first = read_packet(in_order, j * PACKET)
             before = jnp.where(before_last == first, through, 0.0)
         done[j * BODY : (j + 1) * BODY] = before.astype(bf16)
-    for k in range(group):
-        outs[k][...] = done[rows_of(place ^ k, BODY)]
+    for place, out in zip(places, outs):
+        out[...] = done[rows_of(place, BODY)]
 
 
 def start_load(weight_hbm, third, out_ref, sems):
@@ -238,26 +237,19 @@
 def hidden_kernel(group, open_ref, intra_ref, scale_ref, beside_ref, *refs):
     states, (out_ref, in_order) = refs[:group], refs[group:]
     rows, width = open_ref.shape
-    place = place_in(group)
-    for k in range(group):
-        in_order[rows_of(place ^ k, BODY)] = states[k][...]
+    for place, state in zip(helpers(group)[1], states):
+        in_order[rows_of(place, BODY)] = state[...]
     head = lane_head((HD, UC))
     squares = jnp.zeros((rows, LANES), f32)
     for u in range(width // UC):
         cols = slice(u * UC, (u + 1) * UC)
-        pieces = []
-        for s in range(SPLITS):
-            base = (u * SPLITS + s) * BODY
-            pieces.append(
-                jnp.concatenate(
-                    [
-                        in_order[base + c * CUT : base + (c + 1) * CUT]
-                        for c in range(UC // LANES)
-                    ],
-                    axis=1,
-                )
-            )
-        state = jnp.concatenate(pieces, axis=0)
+        state = jnp.concatenate(
+            [
+                in_order[u * BODY + c * HD : u * BODY + (c + 1) * HD]
+                for c in range(UC // LANES)
+            ],
+            axis=1,
+        )
         spread = jnp.concatenate(
             [jnp.where(head == a, state, jnp.zeros((), bf16)) for a in range(UNIT)], axis=0
         )
@@ -294,16 +286,18 @@
         one = ref[:, depth : depth + LANES].astype(f32) + ref[:, depth + LANES :].astype(f32)
         total = one if total is None else total + one
     norm = lax.rsqrt(total / WIDTH + norm_eps)
-    norm = jnp.concatenate([norm] * (wide // LANES), axis=1)
+    norm = jnp.concatenate([norm] * (wide // 2 // LANES), axis=1)
     copies = []
-    for i, weight in enumerate(weights):
-        cols = pl.ds(i * wide, wide)
+    half = wide // 2
+    for i in range(2 * len(weights)):
+        weight, inner = weights[i // 2], pl.ds(i % 2 * half, half)
+        cols = pl.ds(i * half, half)
         value = near_ref[:, cols]
         for k in range(1, parts):
             owner = lax.rem(me + parts - k, parts)
             rows = pl.ds(pl.multiple_of(owner * depth, LANES), depth)
             value = value + jnp.dot(
-                hidden[k][:, :depth], weight[rows], preferred_element_type=f32
+                hidden[k][:, :depth], weight[rows, inner], preferred_element_type=f32
             )
         out_ref[:, cols] = (value * norm).astype(bf16)
         copy = pltpu.make_async_copy(out_ref.at[:, cols], out_hbm.at[:, cols], sems.at[i])
@@ -318,9 +312,14 @@
     features = out_weight.shape[1]
     blocks, parts = lax.axis_size("seq"), lax.axis_size("tp")
     units = width // UC
-    group = units * SPLITS
+    group = units
     back = -(-(-(-(DOC_MOST - 1) // rows)) // group)
-    matchings = [(s, odd) for s in range(1, back + 1) for odd in range(2) if (odd + 1) * s * group < blocks]
+    matchings = [
+        (s, odd)
+        for s in range(1, back + 1)
+        for odd in range(2)
+        if (odd + 1) * s * group < blocks
+    ]
     ids = doc_ids.reshape(1, rows)
     gain = norm_gain.reshape(1, WIDTH)
     dma = pltpu.SemaphoreType.DMA
@@ -331,18 +330,25 @@
     wide = jax.ShapeDtypeStruct((rows, width), f32)
     third = pltpu.VMEM((out_weight.shape[0], features // 3), bf16)
 
-    def swap(value, pairs):
-        return lax.ppermute(value, "seq", pairs)
+    def swap(value, partner):
+        pairs = [
+            (i * parts + t, partner(i, t) * parts + t) for i in range(blocks) for t in range(parts)
+        ]
+        return lax.ppermute(value, ("seq", "tp"), pairs)
 
     def trade(values):
         return [values[0]] + [
-            swap(values[k], [(i, i ^ k) for i in range(blocks)]) for k in range(1, group)
+            swap(values[j], lambda i, t: i ^ orders(group)[t % 2][j]) for j in range(1, group)
         ]
 
     def matching(shift, odd):
         step = shift * group
-        lower = [i for i in range(blocks - step) if (i // step) % 2 == odd]
-        return [(i, i + step) for i in lower] + [(i + step, i) for i in lower]
+
+        def partner(i, t):
+            other = i + step if (i // step) % 2 == odd else i - step
+            return other if 0 <= other < blocks else i
+
+        return partner
 
     def load(index, after):
         return call(
@@ -413,7 +419,7 @@
         [jax.ShapeDtypeStruct((rows, features), bf16)],
         (near, *weights, hidden, *others),
         "far",
-        scratch=[pltpu.VMEM((rows, features), bf16), dma((3,))],
+        scratch=[pltpu.VMEM((rows, features), bf16), dma((6,))],
         far_out=(0,),
         flops=2 * rows * width * features,
         moved=2 * width * features,

time: 33.2 us -> 32.2 us (0.970)
  waiting for transfers between devices: 2.75 us -> 1.77 us
    ppermute x9, waiting for transfers between devices: 2.36 us -> 1.38 us  [swap(): return lax.ppermute(value, ('seq', 'tp'), pairs)]
  transfers between devices with their start and end apart: 10 -> 10, of which waited for: 4 -> 4; matrix products, arithmetic and copies ran while one was open for 0% -> 0% of each run, Pallas kernels for 32% -> 33%
where the time goes in v2:
time: 32.2 us; the launch traced here: 32.1 us
  Pallas kernels  15.7 us (49%)
  starting transfers between devices  14.4 us (45%)
  waiting for transfers between devices  1.77 us (5%)
    pallas_call x9, Pallas kernels, call(): pl.pallas_call(kernel, out_shape=outs, in_specs=[IN_HBM if i in far_in el...  15.7 us
    ppermute x9, starting transfers between devices, swap(): return lax.ppermute(value, ('seq', 'tp'), pairs)  14.4 us
    ppermute x9, waiting for transfers between devices, swap(): return lax.ppermute(value, ('seq', 'tp'), pairs)  1.38 us
  transfers between devices with their start and end apart: 10, of which 4 were waited for; matrix products, arithmetic and copies ran while one was open for 0% of the time, Pallas kernels for 33%

profile of v2, /device:TPU:0, one launch (start us, length us, event | category | flops | bytes accessed | tf_op | source)
XLA Modules:
  0.0 32.1 jit_solution(13758068659153794545)
XLA Ops:
  0.0 2.2 %own_states.1 = (bf16[304,128]{1,0:T(8,128)(2,1)S(1)}, bf16[304,128]{1,0:T(8,128)(2,1)S(1)}, bf16[304,128]{1,0:T(8,128)(2,1)S(1)}, bf16[304,128]{1,0:T(8,128)(2,1)S(1)}) custom-call(bf16[128,1536]{1,0:T(8,128)(2,1)} %key_hbm.3, bf16[128,1536]{1,0:T(8,128)(2,1)} %value_hbm.3, s32[1,128]{1,0:T(1,128)} %bitcast.3), custom_call_target="tpu_custom_call" | custom-call | tf_op jit(solution)/shard_map/own_states/pallas_call | solution.py:34
  2.2 4.0 %collective-permute-start = (bf16[304,128]{1,0:T(8,128)(2,1)S(1)}, bf16[304,128]{1,0:T(8,128)(2,1)S(1)}, u32[]{:S(2)}, u32[]{:S(2)}) collective-permute-start(bf16[304,128]{1,0:T(8,128)(2,1)S(1)} %get-tuple-element.21), channel_id=1, source_target_pairs={{0,6},{1,7},{2,4},{3,5},{4,2},{5,3},{6,0},{7,1},{8,14},{9,15},{10,... | collective-permute-start | bytes 233480 | tf_op jit(solution)/shard_map/ppermute | solution.py:337
  6.2 0.5 %collective-permute-start.1 = (bf16[304,128]{1,0:T(8,128)(2,1)S(1)}, bf16[304,128]{1,0:T(8,128)(2,1)S(1)}, u32[]{:S(2)}, u32[]{:S(2)}) collective-permute-start(bf16[304,128]{1,0:T(8,128)(2,1)S(1)} %get-tuple-element.22), channel_id=1, source_target_pairs={{0,2},{1,5},{2,0},{3,7},{4,6},{5,1},{6,4},{7,3},{8,10},{9,13},{10,... | collective-permute-start | bytes 233480 | tf_op jit(solution)/shard_map/ppermute | solution.py:337
  6.7 0.1 collective-permute-start.2
  6.8 3.4 %intra.1 = (f32[128,1536]{1,0:T(8,128)S(1)}, f32[128,1536]{1,0:T(8,128)S(1)}, bf16[128,1536]{1,0:T(8,128)(2,1)S(1)}, bf16[3072,1024]{1,0:T(8,128)(2,1)S(1)}) custom-call(bf16[304,128]{1,0:T(8,128)(2,1)S(1)} %get-tuple-element.17.after_ref.refs_0_, bf16[128,1536]{1,0:T(8,128)(2,1)} %query_hbm.1, bf16[128,1536]{1,0:T(8,128)(2,1)} %key_hbm.3, ...), custom_call_target="tpu_custom_call" | custom-call | flops 402653184 | bytes 12582912 | tf_op jit(solution)/shard_map/intra/pallas_call | solution.py:34
  10.3 0.0 collective-permute-done.refs_1_
  10.3 0.5 %collective-permute-done.1.refs_2_ = bf16[304,128]{1,0:T(8,128)(2,1)S(1)} collective-permute-done((bf16[304,128]{1,0:T(8,128)(2,1)S(1)}, bf16[304,128]{1,0:T(8,128)(2,1)S(1)}, u32[]{:S(2)}, u32[]{:S(2)}) %collective-permute-start.1) | collective-permute-done | bytes 77856 | tf_op jit(solution)/shard_map/ppermute | solution.py:337
  10.7 0.4 %collective-permute-done.2.refs_3_ = bf16[304,128]{1,0:T(8,128)(2,1)S(1)} collective-permute-done((bf16[304,128]{1,0:T(8,128)(2,1)S(1)}, bf16[304,128]{1,0:T(8,128)(2,1)S(1)}, u32[]{:S(2)}, u32[]{:S(2)}) %collective-permute-start.2) | collective-permute-done | bytes 77856 | tf_op jit(solution)/shard_map/ppermute | solution.py:337
  11.1 0.1 group_state.1.after_ref
  11.2 2.7 %collective-permute-start.5 = (bf16[304,128]{1,0:T(8,128)(2,1)S(1)}, bf16[304,128]{1,0:T(8,128)(2,1)S(1)}, u32[]{:S(2)}, u32[]{:S(2)}) collective-permute-start(bf16[304,128]{1,0:T(8,128)(2,1)S(1)} %group_state.1.after_ref), channel_id=1, source_target_pairs={{0,16},{1,17},{2,18},{3,19},{4,20},{5,21},{6,22},{7,23},{8,24},{9,... | collective-permute-start | bytes 233480 | tf_op jit(solution)/shard_map/ppermute | solution.py:337
  13.8 0.7 %collective-permute-start.4 = (bf16[304,128]{1,0:T(8,128)(2,1)S(1)}, bf16[304,128]{1,0:T(8,128)(2,1)S(1)}, u32[]{:S(2)}, u32[]{:S(2)}) collective-permute-start(bf16[304,128]{1,0:T(8,128)(2,1)S(1)} %group_state.1.after_ref), channel_id=1, source_target_pairs={{0,0},{1,1},{2,2},{3,3},{4,4},{5,5},{6,6},{7,7},{8,16},{9,17},{10,... | collective-permute-start | bytes 233480 | tf_op jit(solution)/shard_map/ppermute | solution.py:337
  14.5 2.9 %collective-permute-start.3 = (bf16[304,128]{1,0:T(8,128)(2,1)S(1)}, bf16[304,128]{1,0:T(8,128)(2,1)S(1)}, u32[]{:S(2)}, u32[]{:S(2)}) collective-permute-start(bf16[304,128]{1,0:T(8,128)(2,1)S(1)} %group_state.1.after_ref), channel_id=1, source_target_pairs={{0,8},{1,9},{2,10},{3,11},{4,12},{5,13},{6,14},{7,15},{8,0},{9,1},... | collective-permute-start | bytes 233480 | tf_op jit(solution)/shard_map/ppermute | solution.py:337
  17.4 2.9 %weight_load.2.beside_ref.refs_1_ = bf16[3072,1024]{1,0:T(8,128)(2,1)S(1)} custom-call(bf16[304,128]{1,0:T(8,128)(2,1)S(1)} %group_state.1.after_ref, bf16[3072,3072]{1,0:T(8,128)(2,1)} %weight_hbm.5), custom_call_target="tpu_custom_call" | custom-call | bytes 12582912 | tf_op jit(solution)/shard_map/weight_load/pallas_call | solution.py:34
  20.3 0.0 collective-permute-done.5.refs_6_
  20.3 0.0 collective-permute-done.4.refs_5_
  20.3 0.0 collective-permute-done.3.refs_4_
  20.3 0.2 prefix_states.1
  20.5 2.1 %collective-permute-start.6 = (bf16[288,128]{1,0:T(8,128)(2,1)S(1)}, bf16[288,128]{1,0:T(8,128)(2,1)S(1)}, u32[]{:S(2)}, u32[]{:S(2)}) collective-permute-start(bf16[288,128]{1,0:T(8,128)(2,1)S(1)} %get-tuple-element.25), channel_id=1, source_target_pairs={{0,6},{1,7},{2,4},{3,5},{4,2},{5,3},{6,0},{7,1},{8,14},{9,15},{10,... | collective-permute-start | bytes 221192 | tf_op jit(solution)/shard_map/ppermute | solution.py:337
  22.6 0.5 %collective-permute-start.7 = (bf16[288,128]{1,0:T(8,128)(2,1)S(1)}, bf16[288,128]{1,0:T(8,128)(2,1)S(1)}, u32[]{:S(2)}, u32[]{:S(2)}) collective-permute-start(bf16[288,128]{1,0:T(8,128)(2,1)S(1)} %get-tuple-element.26), channel_id=1, source_target_pairs={{0,2},{1,5},{2,0},{3,7},{4,6},{5,1},{6,4},{7,3},{8,10},{9,13},{10,... | collective-permute-start | bytes 221192 | tf_op jit(solution)/shard_map/ppermute | solution.py:337
  23.1 0.9 %collective-permute-start.8 = (bf16[288,128]{1,0:T(8,128)(2,1)S(1)}, bf16[288,128]{1,0:T(8,128)(2,1)S(1)}, u32[]{:S(2)}, u32[]{:S(2)}) collective-permute-start(bf16[288,128]{1,0:T(8,128)(2,1)S(1)} %get-tuple-element.27), channel_id=1, source_target_pairs={{0,4},{1,3},{2,6},{3,1},{4,0},{5,7},{6,2},{7,5},{8,12},{9,11},{10,... | collective-permute-start | bytes 221192 | tf_op jit(solution)/shard_map/ppermute | solution.py:337
  24.1 2.9 %weight_load.3.beside_ref.refs_2_ = bf16[3072,1024]{1,0:T(8,128)(2,1)S(1)} custom-call(bf16[288,128]{1,0:T(8,128)(2,1)S(1)} %get-tuple-element.24.after_ref.refs_0_, bf16[3072,3072]{1,0:T(8,128)(2,1)} %weight_hbm.5), custom_call_target="tpu_custom_call" | custom-call | bytes 12582912 | tf_op jit(solution)/shard_map/weight_load/pallas_call | solution.py:34
  26.9 0.0 collective-permute-done.6.refs_1_
  27.0 0.0 collective-permute-done.7.refs_2_
  27.0 0.5 %collective-permute-done.8.refs_3_ = bf16[288,128]{1,0:T(8,128)(2,1)S(1)} collective-permute-done((bf16[288,128]{1,0:T(8,128)(2,1)S(1)}, bf16[288,128]{1,0:T(8,128)(2,1)S(1)}, u32[]{:S(2)}, u32[]{:S(2)}) %collective-permute-start.8) | collective-permute-done | bytes 73760 | tf_op jit(solution)/shard_map/ppermute | solution.py:337
  27.5 0.6 %hidden.1.hidden_ref.refs_3_ = bf16[128,1792]{1,0:T(8,128)(2,1)S(1)} custom-call(bf16[128,1536]{1,0:T(8,128)(2,1)S(1)} %get-tuple-element.18.open_ref, f32[128,1536]{1,0:T(8,128)S(1)} %get-tuple-element.19.beside_ref.intra_ref, f32[128,1536]{1,0:T(8,128)S(1)} %get-tuple-element.20.scale_ref, bf16[3072,1024]{1,0:T(8,128)(2,1)S(1)} %weight_load.3.beside_ref.refs_2_, ...), custom_call_target="tpu_custom_call" | custom-call | tf_op jit(solution)/shard_map/hidden/pallas_call | solution.py:34
  28.1 0.1 collective-permute-start.9
  28.1 1.4 %near.1.near_ref = f32[128,3072]{1,0:T(8,128)S(1)} custom-call(bf16[128,1792]{1,0:T(8,128)(2,1)S(1)} %hidden.1.hidden_ref.refs_3_, bf16[3072,1024]{1,0:T(8,128)(2,1)S(1)} %get-tuple-element.28.refs_0_, bf16[3072,1024]{1,0:T(8,128)(2,1)S(1)} %weight_load.2.beside_ref.refs_1_, bf16[3072,1024]{1,0:T(8,128)(2,1)S(1)} %weight_load.3.beside_ref.refs_2_), custom_call_target="tpu_custom_call" | custom-call | flops 1207959552 | bytes 9437184 | tf_op jit(solution)/shard_map/near/pallas_call | solution.py:34
  29.5 0.4 %collective-permute-done.9.refs_4_ = bf16[128,1792]{1,0:T(8,128)(2,1)S(1)} collective-permute-done((bf16[128,1792]{1,0:T(8,128)(2,1)S(1)}, bf16[128,1792]{1,0:T(8,128)(2,1)S(1)}, u32[]{:S(2)}, u32[]{:S(2)}) %collective-permute-start.9) | collective-permute-done | bytes 458784 | tf_op jit(solution)/shard_map/ppermute | solution.py:405
  29.9 2.1 %far.1 = bf16[128,3072]{1,0:T(8,128)(2,1)} custom-call(f32[128,3072]{1,0:T(8,128)S(1)} %near.1.near_ref, bf16[3072,1024]{1,0:T(8,128)(2,1)S(1)} %get-tuple-element.28.refs_0_, bf16[3072,1024]{1,0:T(8,128)(2,1)S(1)} %weight_load.2.beside_ref.refs_1_, bf16[3072,1024]{1,0:T(8,128)(2,1)S(1)} %weight_load.3.beside_ref.refs_2_, ...), custom_call_target="tpu_custom_call" | custom-call | flops 1207959552 | bytes 9437184 | tf_op jit(solution)/shard_map/far/pallas_call | solution.py:34
Async XLA Ops:
  2.2 8.0 %collective-permute-start = (bf16[304,128]{1,0:T(8,128)(2,1)S(1)}, bf16[304,128]{1,0:T(8,128)(2,1)S(1)}, u32[]{:S(2)}, u32[]{:S(2)}) collective-permute-start(bf16[304,128]{1,0:T(8,128)(2,1)S(1)} %get-tuple-element.21), channel_id=1, source_target_pairs={{0,6},{1,7},{2,4},{3,5},{4,2},{5,3},{6,0},{7,1},{8,14},{9,15},{10,... | collective-permute-start | bytes 233480 | tf_op jit(solution)/shard_map/ppermute | solution.py:337
  6.2 4.6 %collective-permute-start.1 = (bf16[304,128]{1,0:T(8,128)(2,1)S(1)}, bf16[304,128]{1,0:T(8,128)(2,1)S(1)}, u32[]{:S(2)}, u32[]{:S(2)}) collective-permute-start(bf16[304,128]{1,0:T(8,128)(2,1)S(1)} %get-tuple-element.22), channel_id=1, source_target_pairs={{0,2},{1,5},{2,0},{3,7},{4,6},{5,1},{6,4},{7,3},{8,10},{9,13},{10,... | collective-permute-start | bytes 233480 | tf_op jit(solution)/shard_map/ppermute | solution.py:337
  6.7 4.4 %collective-permute-start.2 = (bf16[304,128]{1,0:T(8,128)(2,1)S(1)}, bf16[304,128]{1,0:T(8,128)(2,1)S(1)}, u32[]{:S(2)}, u32[]{:S(2)}) collective-permute-start(bf16[304,128]{1,0:T(8,128)(2,1)S(1)} %get-tuple-element.23), channel_id=1, source_target_pairs={{0,4},{1,3},{2,6},{3,1},{4,0},{5,7},{6,2},{7,5},{8,12},{9,11},{10,... | collective-permute-start | bytes 233480 | tf_op jit(solution)/shard_map/ppermute | solution.py:337
  11.2 9.1 %collective-permute-start.5 = (bf16[304,128]{1,0:T(8,128)(2,1)S(1)}, bf16[304,128]{1,0:T(8,128)(2,1)S(1)}, u32[]{:S(2)}, u32[]{:S(2)}) collective-permute-start(bf16[304,128]{1,0:T(8,128)(2,1)S(1)} %group_state.1.after_ref), channel_id=1, source_target_pairs={{0,16},{1,17},{2,18},{3,19},{4,20},{5,21},{6,22},{7,23},{8,24},{9,... | collective-permute-start | bytes 233480 | tf_op jit(solution)/shard_map/ppermute | solution.py:337
  13.8 6.5 %collective-permute-start.4 = (bf16[304,128]{1,0:T(8,128)(2,1)S(1)}, bf16[304,128]{1,0:T(8,128)(2,1)S(1)}, u32[]{:S(2)}, u32[]{:S(2)}) collective-permute-start(bf16[304,128]{1,0:T(8,128)(2,1)S(1)} %group_state.1.after_ref), channel_id=1, source_target_pairs={{0,0},{1,1},{2,2},{3,3},{4,4},{5,5},{6,6},{7,7},{8,16},{9,17},{10,... | collective-permute-start | bytes 233480 | tf_op jit(solution)/shard_map/ppermute | solution.py:337
  14.5 5.8 %collective-permute-start.3 = (bf16[304,128]{1,0:T(8,128)(2,1)S(1)}, bf16[304,128]{1,0:T(8,128)(2,1)S(1)}, u32[]{:S(2)}, u32[]{:S(2)}) collective-permute-start(bf16[304,128]{1,0:T(8,128)(2,1)S(1)} %group_state.1.after_ref), channel_id=1, source_target_pairs={{0,8},{1,9},{2,10},{3,11},{4,12},{5,13},{6,14},{7,15},{8,0},{9,1},... | collective-permute-start | bytes 233480 | tf_op jit(solution)/shard_map/ppermute | solution.py:337
  20.5 6.4 %collective-permute-start.6 = (bf16[288,128]{1,0:T(8,128)(2,1)S(1)}, bf16[288,128]{1,0:T(8,128)(2,1)S(1)}, u32[]{:S(2)}, u32[]{:S(2)}) collective-permute-start(bf16[288,128]{1,0:T(8,128)(2,1)S(1)} %get-tuple-element.25), channel_id=1, source_target_pairs={{0,6},{1,7},{2,4},{3,5},{4,2},{5,3},{6,0},{7,1},{8,14},{9,15},{10,... | collective-permute-start | bytes 221192 | tf_op jit(solution)/shard_map/ppermute | solution.py:337
  22.6 4.4 %collective-permute-start.7 = (bf16[288,128]{1,0:T(8,128)(2,1)S(1)}, bf16[288,128]{1,0:T(8,128)(2,1)S(1)}, u32[]{:S(2)}, u32[]{:S(2)}) collective-permute-start(bf16[288,128]{1,0:T(8,128)(2,1)S(1)} %get-tuple-element.26), channel_id=1, source_target_pairs={{0,2},{1,5},{2,0},{3,7},{4,6},{5,1},{6,4},{7,3},{8,10},{9,13},{10,... | collective-permute-start | bytes 221192 | tf_op jit(solution)/shard_map/ppermute | solution.py:337
  23.1 4.4 %collective-permute-start.8 = (bf16[288,128]{1,0:T(8,128)(2,1)S(1)}, bf16[288,128]{1,0:T(8,128)(2,1)S(1)}, u32[]{:S(2)}, u32[]{:S(2)}) collective-permute-start(bf16[288,128]{1,0:T(8,128)(2,1)S(1)} %get-tuple-element.27), channel_id=1, source_target_pairs={{0,4},{1,3},{2,6},{3,1},{4,0},{5,7},{6,2},{7,5},{8,12},{9,11},{10,... | collective-permute-start | bytes 221192 | tf_op jit(solution)/shard_map/ppermute | solution.py:337
  28.1 1.9 %collective-permute-start.9 = (bf16[128,1792]{1,0:T(8,128)(2,1)S(1)}, bf16[128,1792]{1,0:T(8,128)(2,1)S(1)}, u32[]{:S(2)}, u32[]{:S(2)}) collective-permute-start(bf16[128,1792]{1,0:T(8,128)(2,1)S(1)} %hidden.1.hidden_ref.refs_3_), channel_id=1, source_target_pairs={{0,1},{1,0},{2,3},{3,2},{4,5},{5,4},{6,7},{7,6},{8,9},{9,8},{10,11... | collective-permute-start | bytes 1376264 | tf_op jit(solution)/shard_map/ppermute | solution.py:405

commit v3 on v2

--- a/solution.py
+++ b/solution.py
@@ -17,7 +17,7 @@
 BODY = HD * (UC // LANES)
 IDS = 16
 PACKET = BODY + IDS
-LOADS = 4
+LOADS = 8
 norm_eps = 1e-05
 
 bf16 = jnp.bfloat16
@@ -173,28 +173,37 @@
     )
 
 
-def load_kernel(third, after_ref, weight_hbm, out_ref, sems):
-    for copy in start_load(weight_hbm, third, out_ref, sems):
+def gate_kernel(
+    after_ref, gate_hbm, gain_hbm, weight_hbm,
+    scale_ref, weight_ref,
+    gate_ref, gain_ref, sems, load_sems,
+):
+    width = gate_ref.shape[1]
+    copies = fetch([(gate_hbm, gate_ref), (gain_hbm, gain_ref)], sems)
+    loads = start_load(weight_hbm, 1, weight_ref, load_sems)
+    part = lax.axis_index("tp")
+    for copy in copies:
         copy.wait()
+    for u in range(width // UC):
+        cols = slice(u * UC, (u + 1) * UC)
+        gain = gain_ref[:, pl.ds(pl.multiple_of(part * width + u * UC, LANES), UC)]
+        scale_ref[:, cols] = gain * jax.nn.sigmoid(gate_ref[:, cols].astype(f32))
+    for load in loads:
+        load.wait()
+
+
+def load_kernel(after_ref, weight_hbm, out_ref, sems):
+    for copy in start_load(weight_hbm, 2, out_ref, sems):
+        copy.wait()
 
 
 def intra_kernel(
-    after_ref, query_hbm, key_hbm, value_hbm, gate_hbm, gain_hbm, doc_hbm, weight_hbm,
-    intra_ref, scale_ref, open_ref, weight_ref,
-    query_ref, key_ref, value_ref, gate_ref, gain_ref, doc_ref, sems, load_sems,
+    after_ref, key_ref, value_ref, query_hbm, doc_hbm, weight_hbm,
+    intra_ref, open_ref, weight_ref,
+    query_ref, doc_ref, sems, load_sems,
 ):
     rows, width = query_ref.shape
-    copies = fetch(
-        [
-            (doc_hbm, doc_ref),
-            (query_hbm, query_ref),
-            (key_hbm, key_ref),
-            (value_hbm, value_ref),
-            (gain_hbm, gain_ref),
-            (gate_hbm, gate_ref),
-        ],
-        sems,
-    )
+    copies = fetch([(doc_hbm, doc_ref), (query_hbm, query_ref)], sems)
     loads = start_load(weight_hbm, 0, weight_ref, load_sems)
     copies[0].wait()
     ids = doc_ref[...].astype(f32)
@@ -206,9 +215,7 @@
     opened = column == jnp.min(ids, axis=1, keepdims=True)
     opened = jnp.concatenate([opened] * (UC // rows), axis=1)
     head = lane_head((rows, UC))
-    part = lax.axis_index("tp")
-    for copy in copies[1:4]:
-        copy.wait()
+    copies[1].wait()
     for u in range(width // UC):
         cols = slice(u * UC, (u + 1) * UC)
         query = query_ref[:, cols]
@@ -224,12 +231,6 @@
         intra_ref[:, cols] = diagonal(
             [mixed[a * rows : (a + 1) * rows] for a in range(UNIT)], head
         )
-    copies[4].wait()
-    copies[5].wait()
-    for u in range(width // UC):
-        cols = slice(u * UC, (u + 1) * UC)
-        gain = gain_ref[:, pl.ds(pl.multiple_of(part * width + u * UC, LANES), UC)]
-        scale_ref[:, cols] = gain * jax.nn.sigmoid(gate_ref[:, cols].astype(f32))
     for load in loads:
         load.wait()
 
@@ -279,19 +280,18 @@
 def far_kernel(parts, near_ref, *refs):
     weights, hidden, (out_hbm, out_ref, sems) = refs[:3], refs[3:-3], refs[-3:]
     depth = hidden[0].shape[1] - 2 * LANES
-    wide = weights[0].shape[1]
+    step = out_ref.shape[1] // 6
     me = lax.axis_index("tp")
     total = None
     for ref in hidden:
         one = ref[:, depth : depth + LANES].astype(f32) + ref[:, depth + LANES :].astype(f32)
         total = one if total is None else total + one
     norm = lax.rsqrt(total / WIDTH + norm_eps)
-    norm = jnp.concatenate([norm] * (wide // 2 // LANES), axis=1)
+    norm = jnp.concatenate([norm] * (step // LANES), axis=1)
     copies = []
-    half = wide // 2
-    for i in range(2 * len(weights)):
-        weight, inner = weights[i // 2], pl.ds(i % 2 * half, half)
-        cols = pl.ds(i * half, half)
+    pieces = [(w, c) for w in weights for c in range(0, w.shape[1], step)]
+    for i, (weight, column) in enumerate(pieces):
+        inner, cols = pl.ds(column, step), pl.ds(i * step, step)
         value = near_ref[:, cols]
         for k in range(1, parts):
             owner = lax.rem(me + parts - k, parts)
@@ -316,19 +316,20 @@
     back = -(-(-(-(DOC_MOST - 1) // rows)) // group)
     matchings = [
         (s, odd)
+        for odd in (0, 1)
         for s in range(1, back + 1)
-        for odd in range(2)
         if (odd + 1) * s * group < blocks
     ]
     ids = doc_ids.reshape(1, rows)
     gain = norm_gain.reshape(1, WIDTH)
     dma = pltpu.SemaphoreType.DMA
-    block16 = pltpu.VMEM((rows, width), bf16)
     ids_block = pltpu.VMEM((1, rows), jnp.int32)
     packet = jax.ShapeDtypeStruct((PACKET, LANES), bf16)
     body = jax.ShapeDtypeStruct((BODY, LANES), bf16)
     wide = jax.ShapeDtypeStruct((rows, width), f32)
+    narrow = jax.ShapeDtypeStruct((rows, width), bf16)
     third = pltpu.VMEM((out_weight.shape[0], features // 3), bf16)
+    moved = 4 * out_weight.size // 3
 
     def swap(value, partner):
         pairs = [
@@ -350,41 +351,43 @@
 
         return partner
 
-    def load(index, after):
-        return call(
-            functools.partial(load_kernel, index),
-            [third],
-            (after, out_weight),
-            "weight_load",
-            scratch=[dma((LOADS,))],
-            far_in=(1,),
-            moved=2 * out_weight.size * 2 // 3,
-        )[0]
-
-    own = call(
+    *own, key_block, value_block = call(
         functools.partial(own_kernel, group),
-        [packet] * group,
+        [packet] * group + [narrow] * 2,
         (key_rows, value_rows, ids),
         "own_states",
-        scratch=[block16, block16, ids_block, dma((1 + 2 * units,))],
+        scratch=[ids_block, dma((1 + 2 * units,))],
         far_in=(0, 1, 2),
     )
     packets = trade(own)
-    intra, scale, opened, weight0 = call(
+    intra, opened, weight0 = call(
         intra_kernel,
-        [wide, wide, jax.ShapeDtypeStruct((rows, width), bf16), third],
-        (own[0], queries, key_rows, value_rows, gate_input, gain, ids, out_weight),
+        [wide, narrow, third],
+        (own[0], key_block, value_block, queries, ids, out_weight),
         "intra",
-        scratch=[block16] * 4 + [pltpu.VMEM((1, WIDTH), f32), ids_block, dma((6,)), dma((LOADS,))],
-        far_in=range(1, 8),
+        scratch=[pltpu.VMEM((rows, width), bf16), ids_block, dma((2,)), dma((LOADS,))],
+        far_in=(3, 4, 5),
         flops=4 * rows * rows * UNIT * width,
-        moved=2 * out_weight.size * 2 // 3,
+        moved=moved,
     )
     (summed,) = call(
         functools.partial(group_kernel, group), [packet], (intra, *packets), "group_state"
     )
     earlier = [swap(summed, matching(s, odd)) for s, odd in matchings]
-    weight1 = load(1, summed)
+    scale, weight1 = call(
+        gate_kernel,
+        [wide, third],
+        (summed, gate_input, gain, out_weight),
+        "gate",
+        scratch=[
+            pltpu.VMEM((rows, width), bf16),
+            pltpu.VMEM((1, WIDTH), f32),
+            dma((2,)),
+            dma((LOADS,)),
+        ],
+        far_in=(1, 2, 3),
+        moved=moved,
+    )
     prefixes = call(
         functools.partial(prefix_kernel, group, matchings),
         [body] * group,
@@ -393,7 +396,15 @@
         scratch=[pltpu.VMEM((group * PACKET, LANES), bf16), pltpu.VMEM((group * BODY, LANES), bf16)],
     )
     states = trade(prefixes)
-    weight2 = load(2, prefixes[0])
+    (weight2,) = call(
+        load_kernel,
+        [third],
+        (prefixes[0], out_weight),
+        "weight_load",
+        scratch=[dma((LOADS,))],
+        far_in=(1,),
+        moved=moved,
+    )
     (hidden,) = call(
         functools.partial(hidden_kernel, group),
         [jax.ShapeDtypeStruct((rows, width + 2 * LANES), bf16)],
@@ -405,11 +416,10 @@
         lax.ppermute(hidden, "tp", [(i, (i + k) % parts) for i in range(parts)])
         for k in range(1, parts)
     ]
-    weights = (weight0, weight1, weight2)
     (near,) = call(
         near_kernel,
         [jax.ShapeDtypeStruct((rows, features), f32)],
-        (hidden, *weights),
+        (hidden, weight0, weight1, weight2),
         "near",
         flops=2 * rows * width * features,
         moved=2 * width * features,
@@ -417,7 +427,7 @@
     (out,) = call(
         functools.partial(far_kernel, parts),
         [jax.ShapeDtypeStruct((rows, features), bf16)],
-        (near, *weights, hidden, *others),
+        (near, weight0, weight1, weight2, hidden, *others),
         "far",
         scratch=[pltpu.VMEM((rows, features), bf16), dma((6,))],
         far_out=(0,),

time: 32.2 us -> 33.4 us (1.037)
  waiting for transfers between devices: 1.77 us -> 3.19 us
  starting transfers between devices: 14.4 us -> 13.6 us
  Pallas kernels: 15.7 us -> 16.4 us
    ppermute x9, waiting for transfers between devices: 1.38 us -> 2.8 us  [swap(): return lax.ppermute(value, ('seq', 'tp'), pairs)]
    ppermute x9, starting transfers between devices: 14.4 us -> 13.5 us  [swap(): return lax.ppermute(value, ('seq', 'tp'), pairs)]
    pallas_call x9, Pallas kernels: 15.7 us -> 16.4 us  [call(): pl.pallas_call(kernel, out_shape=outs, in_specs=[IN_HBM if i in far_in el...]
  transfers between devices with their start and end apart: 10 -> 10, of which waited for: 4 -> 6; matrix products, arithmetic and copies ran while one was open for 0% -> 0% of each run, Pallas kernels for 33% -> 34%
where the time goes in v3:
time: 33.4 us; the launch traced here: 33.3 us
  Pallas kernels  16.4 us (49%)
  starting transfers between devices  13.6 us (41%)
  waiting for transfers between devices  3.19 us (10%)
    pallas_call x9, Pallas kernels, call(): pl.pallas_call(kernel, out_shape=outs, in_specs=[IN_HBM if i in far_in el...  16.4 us
    ppermute x9, starting transfers between devices, swap(): return lax.ppermute(value, ('seq', 'tp'), pairs)  13.5 us
    ppermute x9, waiting for transfers between devices, swap(): return lax.ppermute(value, ('seq', 'tp'), pairs)  2.8 us
  transfers between devices with their start and end apart: 10, of which 6 were waited for; matrix products, arithmetic and copies ran while one was open for 0% of the time, Pallas kernels for 34%

profile of v3, /device:TPU:0, one launch (start us, length us, event | category | flops | bytes accessed | tf_op | source)
XLA Modules:
  0.0 33.3 jit_solution(15027793228749313327)
XLA Ops:
  0.0 2.2 %own_states.1 = (bf16[304,128]{1,0:T(8,128)(2,1)S(1)}, bf16[304,128]{1,0:T(8,128)(2,1)S(1)}, bf16[304,128]{1,0:T(8,128)(2,1)S(1)}, bf16[304,128]{1,0:T(8,128)(2,...) custom-call(bf16[128,1536]{1,0:T(8,128)(2,1)} %key_hbm.1, bf16[128,1536]{1,0:T(8,128)(2,1)} %value_hbm.1, ...), custom_call_target="tpu_custom_call" | custom-call | tf_op jit(solution)/shard_map/own_states/pallas_call | solution.py:34
  2.2 4.0 %collective-permute-start = (bf16[304,128]{1,0:T(8,128)(2,1)S(1)}, bf16[304,128]{1,0:T(8,128)(2,1)S(1)}, u32[]{:S(2)}, u32[]{:S(2)}) collective-permute-start(bf16[304,128]{1,0:T(8,128)(2,1)S(1)} %get-tuple-element.25), channel_id=1, source_target_pairs={{0,6},{1,7},{2,4},{3,5},{4,2},{5,3},{6,0},{7,1},{8,14},{9,15},{10,... | collective-permute-start | bytes 233480 | tf_op jit(solution)/shard_map/ppermute | solution.py:338
  6.2 0.5 %collective-permute-start.1 = (bf16[304,128]{1,0:T(8,128)(2,1)S(1)}, bf16[304,128]{1,0:T(8,128)(2,1)S(1)}, u32[]{:S(2)}, u32[]{:S(2)}) collective-permute-start(bf16[304,128]{1,0:T(8,128)(2,1)S(1)} %get-tuple-element.26), channel_id=1, source_target_pairs={{0,2},{1,5},{2,0},{3,7},{4,6},{5,1},{6,4},{7,3},{8,10},{9,13},{10,... | collective-permute-start | bytes 233480 | tf_op jit(solution)/shard_map/ppermute | solution.py:338
  6.7 0.1 collective-permute-start.2
  6.8 4.0 %intra.1 = (f32[128,1536]{1,0:T(8,128)S(1)}, bf16[128,1536]{1,0:T(8,128)(2,1)S(1)}, bf16[3072,1024]{1,0:T(8,128)(2,1)S(1)}) custom-call(bf16[304,128]{1,0:T(8,128)(2,1)S(1)} %get-tuple-element.20.after_ref.refs_0_, bf16[128,1536]{1,0:T(8,128)(2,1)S(1)} %get-tuple-element.21.key_ref, bf16[128,1536]{1,0:T(8,128)(2,1)S(1)} %get-tuple-element.22.value_ref, ...), custom_call_target="tpu_custom_call" | custom-call | flops 402653184 | bytes 12582912 | tf_op jit(solution)/shard_map/intra/pallas_call | solution.py:34
  10.8 0.0 collective-permute-done.refs_1_
  10.8 0.0 collective-permute-done.1.refs_2_
  10.8 0.3 collective-permute-done.2.refs_3_
  11.1 0.1 group_state.1.after_ref
  11.2 0.7 %collective-permute-start.5 = (bf16[304,128]{1,0:T(8,128)(2,1)S(1)}, bf16[304,128]{1,0:T(8,128)(2,1)S(1)}, u32[]{:S(2)}, u32[]{:S(2)}) collective-permute-start(bf16[304,128]{1,0:T(8,128)(2,1)S(1)} %group_state.1.after_ref), channel_id=1, source_target_pairs={{0,0},{1,1},{2,2},{3,3},{4,4},{5,5},{6,6},{7,7},{8,16},{9,17},{10,... | collective-permute-start | bytes 233480 | tf_op jit(solution)/shard_map/ppermute | solution.py:338
  11.8 4.5 %collective-permute-start.4 = (bf16[304,128]{1,0:T(8,128)(2,1)S(1)}, bf16[304,128]{1,0:T(8,128)(2,1)S(1)}, u32[]{:S(2)}, u32[]{:S(2)}) collective-permute-start(bf16[304,128]{1,0:T(8,128)(2,1)S(1)} %group_state.1.after_ref), channel_id=1, source_target_pairs={{0,16},{1,17},{2,18},{3,19},{4,20},{5,21},{6,22},{7,23},{8,24},{9,... | collective-permute-start | bytes 233480 | tf_op jit(solution)/shard_map/ppermute | solution.py:338
  16.3 0.2 collective-permute-start.3
  16.5 3.0 %gate.1 = (f32[128,1536]{1,0:T(8,128)S(1)}, bf16[3072,1024]{1,0:T(8,128)(2,1)S(1)}) custom-call(bf16[304,128]{1,0:T(8,128)(2,1)S(1)} %group_state.1.after_ref, bf16[128,1536]{1,0:T(8,128)(2,1)} %gate_hbm.1, f32[1,3072]{1,0:T(1,128)} %bitcast.2, bf16[3072,3072]{1,0:T(8,128)(2,1)} %weight_hbm.5), custom_call_target="tpu_custom_call" | custom-call | bytes 12582912 | tf_op jit(solution)/shard_map/gate/pallas_call | solution.py:34
  19.5 0.0 collective-permute-done.5.refs_6_
  19.6 0.8 %collective-permute-done.4.refs_5_ = bf16[304,128]{1,0:T(8,128)(2,1)S(1)} collective-permute-done((bf16[304,128]{1,0:T(8,128)(2,1)S(1)}, bf16[304,128]{1,0:T(8,128)(2,1)S(1)}, u32[]{:S(2)}, u32[]{:S(2)}) %collective-permute-start.4) | collective-permute-done | bytes 77856 | tf_op jit(solution)/shard_map/ppermute | solution.py:338
  20.3 0.8 %collective-permute-done.3.refs_4_ = bf16[304,128]{1,0:T(8,128)(2,1)S(1)} collective-permute-done((bf16[304,128]{1,0:T(8,128)(2,1)S(1)}, bf16[304,128]{1,0:T(8,128)(2,1)S(1)}, u32[]{:S(2)}, u32[]{:S(2)}) %collective-permute-start.3) | collective-permute-done | bytes 77856 | tf_op jit(solution)/shard_map/ppermute | solution.py:338
  21.1 0.2 prefix_states.1
  21.3 2.5 %collective-permute-start.6 = (bf16[288,128]{1,0:T(8,128)(2,1)S(1)}, bf16[288,128]{1,0:T(8,128)(2,1)S(1)}, u32[]{:S(2)}, u32[]{:S(2)}) collective-permute-start(bf16[288,128]{1,0:T(8,128)(2,1)S(1)} %get-tuple-element.31), channel_id=1, source_target_pairs={{0,6},{1,7},{2,4},{3,5},{4,2},{5,3},{6,0},{7,1},{8,14},{9,15},{10,... | collective-permute-start | bytes 221192 | tf_op jit(solution)/shard_map/ppermute | solution.py:338
  23.8 0.5 %collective-permute-start.7 = (bf16[288,128]{1,0:T(8,128)(2,1)S(1)}, bf16[288,128]{1,0:T(8,128)(2,1)S(1)}, u32[]{:S(2)}, u32[]{:S(2)}) collective-permute-start(bf16[288,128]{1,0:T(8,128)(2,1)S(1)} %get-tuple-element.32), channel_id=1, source_target_pairs={{0,2},{1,5},{2,0},{3,7},{4,6},{5,1},{6,4},{7,3},{8,10},{9,13},{10,... | collective-permute-start | bytes 221192 | tf_op jit(solution)/shard_map/ppermute | solution.py:338
  24.3 0.5 %collective-permute-start.8 = (bf16[288,128]{1,0:T(8,128)(2,1)S(1)}, bf16[288,128]{1,0:T(8,128)(2,1)S(1)}, u32[]{:S(2)}, u32[]{:S(2)}) collective-permute-start(bf16[288,128]{1,0:T(8,128)(2,1)S(1)} %get-tuple-element.33), channel_id=1, source_target_pairs={{0,4},{1,3},{2,6},{3,1},{4,0},{5,7},{6,2},{7,5},{8,12},{9,11},{10,... | collective-permute-start | bytes 221192 | tf_op jit(solution)/shard_map/ppermute | solution.py:338
  24.9 2.9 %weight_load.1.beside_ref.refs_2_ = bf16[3072,1024]{1,0:T(8,128)(2,1)S(1)} custom-call(bf16[288,128]{1,0:T(8,128)(2,1)S(1)} %get-tuple-element.30.after_ref.refs_0_, bf16[3072,3072]{1,0:T(8,128)(2,1)} %weight_hbm.5), custom_call_target="tpu_custom_call" | custom-call | bytes 12582912 | tf_op jit(solution)/shard_map/weight_load/pallas_call | solution.py:34
  27.7 0.0 collective-permute-done.6.refs_1_
  27.7 0.4 %collective-permute-done.7.refs_2_ = bf16[288,128]{1,0:T(8,128)(2,1)S(1)} collective-permute-done((bf16[288,128]{1,0:T(8,128)(2,1)S(1)}, bf16[288,128]{1,0:T(8,128)(2,1)S(1)}, u32[]{:S(2)}, u32[]{:S(2)}) %collective-permute-start.7) | collective-permute-done | bytes 73760 | tf_op jit(solution)/shard_map/ppermute | solution.py:338
  28.2 0.5 %collective-permute-done.8.refs_3_ = bf16[288,128]{1,0:T(8,128)(2,1)S(1)} collective-permute-done((bf16[288,128]{1,0:T(8,128)(2,1)S(1)}, bf16[288,128]{1,0:T(8,128)(2,1)S(1)}, u32[]{:S(2)}, u32[]{:S(2)}) %collective-permute-start.8) | collective-permute-done | bytes 73760 | tf_op jit(solution)/shard_map/ppermute | solution.py:338
  28.7 0.6 %hidden.1.hidden_ref.refs_3_ = bf16[128,1792]{1,0:T(8,128)(2,1)S(1)} custom-call(bf16[128,1536]{1,0:T(8,128)(2,1)S(1)} %get-tuple-element.23.open_ref, f32[128,1536]{1,0:T(8,128)S(1)} %get-tuple-element.24.beside_ref.intra_ref, f32[128,1536]{1,0:T(8,128)S(1)} %get-tuple-element.28.scale_ref, bf16[3072,1024]{1,0:T(8,128)(2,1)S(1)} %weight_load.1.beside_ref.refs_2_, ...), custom_call_target="tpu_custom_call" | custom-call | tf_op jit(solution)/shard_map/hidden/pallas_call | solution.py:34
  29.3 0.1 collective-permute-start.9
  29.4 1.4 %near.1.near_ref = f32[128,3072]{1,0:T(8,128)S(1)} custom-call(bf16[128,1792]{1,0:T(8,128)(2,1)S(1)} %hidden.1.hidden_ref.refs_3_, bf16[3072,1024]{1,0:T(8,128)(2,1)S(1)} %get-tuple-element.34.refs_0_, bf16[3072,1024]{1,0:T(8,128)(2,1)S(1)} %get-tuple-element.29.beside_ref.refs_1_, bf16[3072,1024]{1,0:T(8,128)(2,1)S(1)} %weight_load.1.beside_ref.refs_2_), custom_call_target="tpu_custom_call" | custom-call | flops 1207959552 | bytes 9437184 | tf_op jit(solution)/shard_map/near/pallas_call | solution.py:34
  30.8 0.4 %collective-permute-done.9.refs_4_ = bf16[128,1792]{1,0:T(8,128)(2,1)S(1)} collective-permute-done((bf16[128,1792]{1,0:T(8,128)(2,1)S(1)}, bf16[128,1792]{1,0:T(8,128)(2,1)S(1)}, u32[]{:S(2)}, u32[]{:S(2)}) %collective-permute-start.9) | collective-permute-done | bytes 458784 | tf_op jit(solution)/shard_map/ppermute | solution.py:416
  31.2 2.1 %far.1 = bf16[128,3072]{1,0:T(8,128)(2,1)} custom-call(f32[128,3072]{1,0:T(8,128)S(1)} %near.1.near_ref, bf16[3072,1024]{1,0:T(8,128)(2,1)S(1)} %get-tuple-element.34.refs_0_, bf16[3072,1024]{1,0:T(8,128)(2,1)S(1)} %get-tuple-element.29.beside_ref.refs_1_, bf16[3072,1024]{1,0:T(8,128)(2,1)S(1)} %weight_load.1.beside_ref.refs_2_, ...), custom_call_target="tpu_custom_call" | custom-call | flops 1207959552 | bytes 9437184 | tf_op jit(solution)/shard_map/far/pallas_call | solution.py:34
Async XLA Ops:
  2.2 8.6 %collective-permute-start = (bf16[304,128]{1,0:T(8,128)(2,1)S(1)}, bf16[304,128]{1,0:T(8,128)(2,1)S(1)}, u32[]{:S(2)}, u32[]{:S(2)}) collective-permute-start(bf16[304,128]{1,0:T(8,128)(2,1)S(1)} %get-tuple-element.25), channel_id=1, source_target_pairs={{0,6},{1,7},{2,4},{3,5},{4,2},{5,3},{6,0},{7,1},{8,14},{9,15},{10,... | collective-permute-start | bytes 233480 | tf_op jit(solution)/shard_map/ppermute | solution.py:338
  6.2 4.6 %collective-permute-start.1 = (bf16[304,128]{1,0:T(8,128)(2,1)S(1)}, bf16[304,128]{1,0:T(8,128)(2,1)S(1)}, u32[]{:S(2)}, u32[]{:S(2)}) collective-permute-start(bf16[304,128]{1,0:T(8,128)(2,1)S(1)} %get-tuple-element.26), channel_id=1, source_target_pairs={{0,2},{1,5},{2,0},{3,7},{4,6},{5,1},{6,4},{7,3},{8,10},{9,13},{10,... | collective-permute-start | bytes 233480 | tf_op jit(solution)/shard_map/ppermute | solution.py:338
  6.7 4.4 %collective-permute-start.2 = (bf16[304,128]{1,0:T(8,128)(2,1)S(1)}, bf16[304,128]{1,0:T(8,128)(2,1)S(1)}, u32[]{:S(2)}, u32[]{:S(2)}) collective-permute-start(bf16[304,128]{1,0:T(8,128)(2,1)S(1)} %get-tuple-element.27), channel_id=1, source_target_pairs={{0,4},{1,3},{2,6},{3,1},{4,0},{5,7},{6,2},{7,5},{8,12},{9,11},{10,... | collective-permute-start | bytes 233480 | tf_op jit(solution)/shard_map/ppermute | solution.py:338
  11.2 8.4 %collective-permute-start.5 = (bf16[304,128]{1,0:T(8,128)(2,1)S(1)}, bf16[304,128]{1,0:T(8,128)(2,1)S(1)}, u32[]{:S(2)}, u32[]{:S(2)}) collective-permute-start(bf16[304,128]{1,0:T(8,128)(2,1)S(1)} %group_state.1.after_ref), channel_id=1, source_target_pairs={{0,0},{1,1},{2,2},{3,3},{4,4},{5,5},{6,6},{7,7},{8,16},{9,17},{10,... | collective-permute-start | bytes 233480 | tf_op jit(solution)/shard_map/ppermute | solution.py:338
  11.8 8.5 %collective-permute-start.4 = (bf16[304,128]{1,0:T(8,128)(2,1)S(1)}, bf16[304,128]{1,0:T(8,128)(2,1)S(1)}, u32[]{:S(2)}, u32[]{:S(2)}) collective-permute-start(bf16[304,128]{1,0:T(8,128)(2,1)S(1)} %group_state.1.after_ref), channel_id=1, source_target_pairs={{0,16},{1,17},{2,18},{3,19},{4,20},{5,21},{6,22},{7,23},{8,24},{9,... | collective-permute-start | bytes 233480 | tf_op jit(solution)/shard_map/ppermute | solution.py:338
  16.3 4.8 %collective-permute-start.3 = (bf16[304,128]{1,0:T(8,128)(2,1)S(1)}, bf16[304,128]{1,0:T(8,128)(2,1)S(1)}, u32[]{:S(2)}, u32[]{:S(2)}) collective-permute-start(bf16[304,128]{1,0:T(8,128)(2,1)S(1)} %group_state.1.after_ref), channel_id=1, source_target_pairs={{0,8},{1,9},{2,10},{3,11},{4,12},{5,13},{6,14},{7,15},{8,0},{9,1},... | collective-permute-start | bytes 233480 | tf_op jit(solution)/shard_map/ppermute | solution.py:338
  21.3 6.4 %collective-permute-start.6 = (bf16[288,128]{1,0:T(8,128)(2,1)S(1)}, bf16[288,128]{1,0:T(8,128)(2,1)S(1)}, u32[]{:S(2)}, u32[]{:S(2)}) collective-permute-start(bf16[288,128]{1,0:T(8,128)(2,1)S(1)} %get-tuple-element.31), channel_id=1, source_target_pairs={{0,6},{1,7},{2,4},{3,5},{4,2},{5,3},{6,0},{7,1},{8,14},{9,15},{10,... | collective-permute-start | bytes 221192 | tf_op jit(solution)/shard_map/ppermute | solution.py:338
  23.8 4.4 %collective-permute-start.7 = (bf16[288,128]{1,0:T(8,128)(2,1)S(1)}, bf16[288,128]{1,0:T(8,128)(2,1)S(1)}, u32[]{:S(2)}, u32[]{:S(2)}) collective-permute-start(bf16[288,128]{1,0:T(8,128)(2,1)S(1)} %get-tuple-element.32), channel_id=1, source_target_pairs={{0,2},{1,5},{2,0},{3,7},{4,6},{5,1},{6,4},{7,3},{8,10},{9,13},{10,... | collective-permute-start | bytes 221192 | tf_op jit(solution)/shard_map/ppermute | solution.py:338
  24.3 4.4 %collective-permute-start.8 = (bf16[288,128]{1,0:T(8,128)(2,1)S(1)}, bf16[288,128]{1,0:T(8,128)(2,1)S(1)}, u32[]{:S(2)}, u32[]{:S(2)}) collective-permute-start(bf16[288,128]{1,0:T(8,128)(2,1)S(1)} %get-tuple-element.33), channel_id=1, source_target_pairs={{0,4},{1,3},{2,6},{3,1},{4,0},{5,7},{6,2},{7,5},{8,12},{9,11},{10,... | collective-permute-start | bytes 221192 | tf_op jit(solution)/shard_map/ppermute | solution.py:338
  29.3 1.9 %collective-permute-start.9 = (bf16[128,1792]{1,0:T(8,128)(2,1)S(1)}, bf16[128,1792]{1,0:T(8,128)(2,1)S(1)}, u32[]{:S(2)}, u32[]{:S(2)}) collective-permute-start(bf16[128,1792]{1,0:T(8,128)(2,1)S(1)} %hidden.1.hidden_ref.refs_3_), channel_id=1, source_target_pairs={{0,1},{1,0},{2,3},{3,2},{4,5},{5,4},{6,7},{7,6},{8,9},{9,8},{10,11... | collective-permute-start | bytes 1376264 | tf_op jit(solution)/shard_map/ppermute | solution.py:416

commit v4 on v3

--- a/solution.py
+++ b/solution.py
@@ -17,7 +17,7 @@
 BODY = HD * (UC // LANES)
 IDS = 16
 PACKET = BODY + IDS
-LOADS = 8
+LOADS = 4
 norm_eps = 1e-05
 
 bf16 = jnp.bfloat16
@@ -203,7 +203,10 @@
     query_ref, doc_ref, sems, load_sems,
 ):
     rows, width = query_ref.shape
-    copies = fetch([(doc_hbm, doc_ref), (query_hbm, query_ref)], sems)
+    units = [pl.ds(u * UC, UC) for u in range(width // UC)]
+    copies = fetch(
+        [(doc_hbm, doc_ref)] + [(query_hbm.at[:, c], query_ref.at[:, c]) for c in units], sems
+    )
     loads = start_load(weight_hbm, 0, weight_ref, load_sems)
     copies[0].wait()
     ids = doc_ref[...].astype(f32)
@@ -215,9 +218,8 @@
     opened = column == jnp.min(ids, axis=1, keepdims=True)
     opened = jnp.concatenate([opened] * (UC // rows), axis=1)
     head = lane_head((rows, UC))
-    copies[1].wait()
-    for u in range(width // UC):
-        cols = slice(u * UC, (u + 1) * UC)
+    for cols, copy in zip(units, copies[1:]):
+        copy.wait()
         query = query_ref[:, cols]
         open_ref[:, cols] = jnp.where(opened, query, jnp.zeros((), bf16))
         stacked = jnp.concatenate(
@@ -262,13 +264,14 @@
         out_ref[:, cols] = (attn * scale_ref[:, cols]).astype(bf16)
     total = jnp.broadcast_to(jnp.sum(squares, axis=1, keepdims=True), (rows, LANES))
     high = total.astype(bf16)
-    out_ref[:, width : width + LANES] = high
-    out_ref[:, width + LANES :] = (total - high.astype(f32)).astype(bf16)
+    low = (total - high.astype(f32)).astype(bf16)
+    lane = lax.broadcasted_iota(jnp.int32, (rows, LANES), 1)
+    out_ref[:, width:] = jnp.where(lane < LANES // 2, high, low)
 
 
 def near_kernel(hidden_ref, *refs):
     *weights, out_ref = refs
-    depth = hidden_ref.shape[1] - 2 * LANES
+    depth = hidden_ref.shape[1] - LANES
     rows = pl.ds(pl.multiple_of(lax.axis_index("tp") * depth, LANES), depth)
     wide = weights[0].shape[1]
     for i, weight in enumerate(weights):
@@ -279,12 +282,13 @@
 
 def far_kernel(parts, near_ref, *refs):
     weights, hidden, (out_hbm, out_ref, sems) = refs[:3], refs[3:-3], refs[-3:]
-    depth = hidden[0].shape[1] - 2 * LANES
+    depth = hidden[0].shape[1] - LANES
     step = out_ref.shape[1] // 6
     me = lax.axis_index("tp")
     total = None
     for ref in hidden:
-        one = ref[:, depth : depth + LANES].astype(f32) + ref[:, depth + LANES :].astype(f32)
+        one = ref[:, depth:].astype(f32)
+        one = one + pltpu.roll(one, LANES // 2, 1)
         total = one if total is None else total + one
     norm = lax.rsqrt(total / WIDTH + norm_eps)
     norm = jnp.concatenate([norm] * (step // LANES), axis=1)
@@ -316,8 +320,8 @@
     back = -(-(-(-(DOC_MOST - 1) // rows)) // group)
     matchings = [
         (s, odd)
-        for odd in (0, 1)
-        for s in range(1, back + 1)
+        for odd in (1, 0)
+        for s in range(back, 0, -1)
         if (odd + 1) * s * group < blocks
     ]
     ids = doc_ids.reshape(1, rows)
@@ -365,7 +369,7 @@
         [wide, narrow, third],
         (own[0], key_block, value_block, queries, ids, out_weight),
         "intra",
-        scratch=[pltpu.VMEM((rows, width), bf16), ids_block, dma((2,)), dma((LOADS,))],
+        scratch=[pltpu.VMEM((rows, width), bf16), ids_block, dma((1 + units,)), dma((LOADS,))],
         far_in=(3, 4, 5),
         flops=4 * rows * rows * UNIT * width,
         moved=moved,
@@ -407,7 +411,7 @@
     )
     (hidden,) = call(
         functools.partial(hidden_kernel, group),
-        [jax.ShapeDtypeStruct((rows, width + 2 * LANES), bf16)],
+        [jax.ShapeDtypeStruct((rows, width + LANES), bf16)],
         (opened, intra, scale, weight2, *states),
         "hidden",
         scratch=[pltpu.VMEM((group * BODY, LANES), bf16)],

time: 33.4 us -> 31 us (0.928)
  waiting for transfers between devices: 3.19 us -> 1.95 us
  Pallas kernels: 16.4 us -> 15.5 us
  starting transfers between devices: 13.6 us -> 13.1 us
    ppermute x9, waiting for transfers between devices: 2.8 us -> 1.6 us  [swap(): return lax.ppermute(value, ('seq', 'tp'), pairs)]
    pallas_call x9, Pallas kernels: 16.4 us -> 15.5 us  [call(): pl.pallas_call(kernel, out_shape=outs, in_specs=[IN_HBM if i in far_in el...]
    ppermute x9, starting transfers between devices: 13.5 us -> 13 us  [swap(): return lax.ppermute(value, ('seq', 'tp'), pairs)]
  transfers between devices with their start and end apart: 10 -> 10, of which waited for: 6 -> 5; matrix products, arithmetic and copies ran while one was open for 0% -> 0% of each run, Pallas kernels for 34% -> 34%
where the time goes in v4:
time: 31 us; the launch traced here: 30.7 us
  Pallas kernels  15.5 us (50%)
  starting transfers between devices  13.1 us (42%)
  waiting for transfers between devices  1.95 us (6%)
    pallas_call x9, Pallas kernels, call(): pl.pallas_call(kernel, out_shape=outs, in_specs=[IN_HBM if i in far_in el...  15.5 us
    ppermute x9, starting transfers between devices, swap(): return lax.ppermute(value, ('seq', 'tp'), pairs)  13 us
    ppermute x9, waiting for transfers between devices, swap(): return lax.ppermute(value, ('seq', 'tp'), pairs)  1.6 us
  transfers between devices with their start and end apart: 10, of which 5 were waited for; matrix products, arithmetic and copies ran while one was open for 0% of the time, Pallas kernels for 34%

profile of v4, /device:TPU:0, one launch (start us, length us, event | category | flops | bytes accessed | tf_op | source)
XLA Modules:
  0.0 30.7 jit_solution(17435011620125926588)
XLA Ops:
  0.0 2.2 %own_states.1 = (bf16[304,128]{1,0:T(8,128)(2,1)S(1)}, bf16[304,128]{1,0:T(8,128)(2,1)S(1)}, bf16[304,128]{1,0:T(8,128)(2,1)S(1)}, bf16[304,128]{1,0:T(8,128)(2,...) custom-call(bf16[128,1536]{1,0:T(8,128)(2,1)} %key_hbm.1, bf16[128,1536]{1,0:T(8,128)(2,1)} %value_hbm.1, ...), custom_call_target="tpu_custom_call" | custom-call | tf_op jit(solution)/shard_map/own_states/pallas_call | solution.py:34
  2.2 4.0 %collective-permute-start = (bf16[304,128]{1,0:T(8,128)(2,1)S(1)}, bf16[304,128]{1,0:T(8,128)(2,1)S(1)}, u32[]{:S(2)}, u32[]{:S(2)}) collective-permute-start(bf16[304,128]{1,0:T(8,128)(2,1)S(1)} %get-tuple-element.25), channel_id=1, source_target_pairs={{0,6},{1,7},{2,4},{3,5},{4,2},{5,3},{6,0},{7,1},{8,14},{9,15},{10,... | collective-permute-start | bytes 233480 | tf_op jit(solution)/shard_map/ppermute | solution.py:342
  6.2 0.5 %collective-permute-start.1 = (bf16[304,128]{1,0:T(8,128)(2,1)S(1)}, bf16[304,128]{1,0:T(8,128)(2,1)S(1)}, u32[]{:S(2)}, u32[]{:S(2)}) collective-permute-start(bf16[304,128]{1,0:T(8,128)(2,1)S(1)} %get-tuple-element.26), channel_id=1, source_target_pairs={{0,2},{1,5},{2,0},{3,7},{4,6},{5,1},{6,4},{7,3},{8,10},{9,13},{10,... | collective-permute-start | bytes 233480 | tf_op jit(solution)/shard_map/ppermute | solution.py:342
  6.7 0.1 collective-permute-start.2
  6.8 3.1 %intra.1 = (f32[128,1536]{1,0:T(8,128)S(1)}, bf16[128,1536]{1,0:T(8,128)(2,1)S(1)}, bf16[3072,1024]{1,0:T(8,128)(2,1)S(1)}) custom-call(bf16[304,128]{1,0:T(8,128)(2,1)S(1)} %get-tuple-element.20.after_ref.refs_0_, bf16[128,1536]{1,0:T(8,128)(2,1)S(1)} %get-tuple-element.21.key_ref, bf16[128,1536]{1,0:T(8,128)(2,1)S(1)} %get-tuple-element.22.value_ref, ...), custom_call_target="tpu_custom_call" | custom-call | flops 402653184 | bytes 12582912 | tf_op jit(solution)/shard_map/intra/pallas_call | solution.py:34
  9.9 0.0 collective-permute-done.refs_1_
  9.9 0.8 %collective-permute-done.1.refs_2_ = bf16[304,128]{1,0:T(8,128)(2,1)S(1)} collective-permute-done((bf16[304,128]{1,0:T(8,128)(2,1)S(1)}, bf16[304,128]{1,0:T(8,128)(2,1)S(1)}, u32[]{:S(2)}, u32[]{:S(2)}) %collective-permute-start.1) | collective-permute-done | bytes 77856 | tf_op jit(solution)/shard_map/ppermute | solution.py:342
  10.7 0.4 %collective-permute-done.2.refs_3_ = bf16[304,128]{1,0:T(8,128)(2,1)S(1)} collective-permute-done((bf16[304,128]{1,0:T(8,128)(2,1)S(1)}, bf16[304,128]{1,0:T(8,128)(2,1)S(1)}, u32[]{:S(2)}, u32[]{:S(2)}) %collective-permute-start.2) | collective-permute-done | bytes 77856 | tf_op jit(solution)/shard_map/ppermute | solution.py:342
  11.1 0.1 group_state.1.after_ref
  11.2 1.6 %collective-permute-start.5 = (bf16[304,128]{1,0:T(8,128)(2,1)S(1)}, bf16[304,128]{1,0:T(8,128)(2,1)S(1)}, u32[]{:S(2)}, u32[]{:S(2)}) collective-permute-start(bf16[304,128]{1,0:T(8,128)(2,1)S(1)} %group_state.1.after_ref), channel_id=1, source_target_pairs={{0,8},{1,9},{2,10},{3,11},{4,12},{5,13},{6,14},{7,15},{8,0},{9,1},... | collective-permute-start | bytes 233480 | tf_op jit(solution)/shard_map/ppermute | solution.py:342
  12.8 2.6 %collective-permute-start.4 = (bf16[304,128]{1,0:T(8,128)(2,1)S(1)}, bf16[304,128]{1,0:T(8,128)(2,1)S(1)}, u32[]{:S(2)}, u32[]{:S(2)}) collective-permute-start(bf16[304,128]{1,0:T(8,128)(2,1)S(1)} %group_state.1.after_ref), channel_id=1, source_target_pairs={{0,16},{1,17},{2,18},{3,19},{4,20},{5,21},{6,22},{7,23},{8,24},{9,... | collective-permute-start | bytes 233480 | tf_op jit(solution)/shard_map/ppermute | solution.py:342
  15.4 0.7 %collective-permute-start.3 = (bf16[304,128]{1,0:T(8,128)(2,1)S(1)}, bf16[304,128]{1,0:T(8,128)(2,1)S(1)}, u32[]{:S(2)}, u32[]{:S(2)}) collective-permute-start(bf16[304,128]{1,0:T(8,128)(2,1)S(1)} %group_state.1.after_ref), channel_id=1, source_target_pairs={{0,0},{1,1},{2,2},{3,3},{4,4},{5,5},{6,6},{7,7},{8,16},{9,17},{10,... | collective-permute-start | bytes 233480 | tf_op jit(solution)/shard_map/ppermute | solution.py:342
  16.1 3.0 %gate.1 = (f32[128,1536]{1,0:T(8,128)S(1)}, bf16[3072,1024]{1,0:T(8,128)(2,1)S(1)}) custom-call(bf16[304,128]{1,0:T(8,128)(2,1)S(1)} %group_state.1.after_ref, bf16[128,1536]{1,0:T(8,128)(2,1)} %gate_hbm.1, f32[1,3072]{1,0:T(1,128)} %bitcast.2, bf16[3072,3072]{1,0:T(8,128)(2,1)} %weight_hbm.5), custom_call_target="tpu_custom_call" | custom-call | bytes 12582912 | tf_op jit(solution)/shard_map/gate/pallas_call | solution.py:34
  19.1 0.0 collective-permute-done.5.refs_6_
  19.1 0.2 collective-permute-done.4.refs_5_
  19.3 0.0 collective-permute-done.3.refs_4_
  19.3 0.2 prefix_states.1
  19.5 1.8 %collective-permute-start.6 = (bf16[288,128]{1,0:T(8,128)(2,1)S(1)}, bf16[288,128]{1,0:T(8,128)(2,1)S(1)}, u32[]{:S(2)}, u32[]{:S(2)}) collective-permute-start(bf16[288,128]{1,0:T(8,128)(2,1)S(1)} %get-tuple-element.31), channel_id=1, source_target_pairs={{0,6},{1,7},{2,4},{3,5},{4,2},{5,3},{6,0},{7,1},{8,14},{9,15},{10,... | collective-permute-start | bytes 221192 | tf_op jit(solution)/shard_map/ppermute | solution.py:342
  21.3 0.5 %collective-permute-start.7 = (bf16[288,128]{1,0:T(8,128)(2,1)S(1)}, bf16[288,128]{1,0:T(8,128)(2,1)S(1)}, u32[]{:S(2)}, u32[]{:S(2)}) collective-permute-start(bf16[288,128]{1,0:T(8,128)(2,1)S(1)} %get-tuple-element.32), channel_id=1, source_target_pairs={{0,2},{1,5},{2,0},{3,7},{4,6},{5,1},{6,4},{7,3},{8,10},{9,13},{10,... | collective-permute-start | bytes 221192 | tf_op jit(solution)/shard_map/ppermute | solution.py:342
  21.8 1.2 %collective-permute-start.8 = (bf16[288,128]{1,0:T(8,128)(2,1)S(1)}, bf16[288,128]{1,0:T(8,128)(2,1)S(1)}, u32[]{:S(2)}, u32[]{:S(2)}) collective-permute-start(bf16[288,128]{1,0:T(8,128)(2,1)S(1)} %get-tuple-element.33), channel_id=1, source_target_pairs={{0,4},{1,3},{2,6},{3,1},{4,0},{5,7},{6,2},{7,5},{8,12},{9,11},{10,... | collective-permute-start | bytes 221192 | tf_op jit(solution)/shard_map/ppermute | solution.py:342
  23.0 2.9 %weight_load.1.beside_ref.refs_2_ = bf16[3072,1024]{1,0:T(8,128)(2,1)S(1)} custom-call(bf16[288,128]{1,0:T(8,128)(2,1)S(1)} %get-tuple-element.30.after_ref.refs_0_, bf16[3072,3072]{1,0:T(8,128)(2,1)} %weight_hbm.5), custom_call_target="tpu_custom_call" | custom-call | bytes 12582912 | tf_op jit(solution)/shard_map/weight_load/pallas_call | solution.py:34
  25.9 0.0 collective-permute-done.6.refs_1_
  25.9 0.0 collective-permute-done.7.refs_2_
  25.9 0.2 collective-permute-done.8.refs_3_
  26.2 0.6 %hidden.1.hidden_ref.refs_3_ = bf16[128,1664]{1,0:T(8,128)(2,1)S(1)} custom-call(bf16[128,1536]{1,0:T(8,128)(2,1)S(1)} %get-tuple-element.23.open_ref, f32[128,1536]{1,0:T(8,128)S(1)} %get-tuple-element.24.beside_ref.intra_ref, f32[128,1536]{1,0:T(8,128)S(1)} %get-tuple-element.28.scale_ref, bf16[3072,1024]{1,0:T(8,128)(2,1)S(1)} %weight_load.1.beside_ref.refs_2_, ...), custom_call_target="tpu_custom_call" | custom-call | tf_op jit(solution)/shard_map/hidden/pallas_call | solution.py:34
  26.7 0.1 collective-permute-start.9
  26.8 1.4 %near.1.near_ref = f32[128,3072]{1,0:T(8,128)S(1)} custom-call(bf16[128,1664]{1,0:T(8,128)(2,1)S(1)} %hidden.1.hidden_ref.refs_3_, bf16[3072,1024]{1,0:T(8,128)(2,1)S(1)} %get-tuple-element.34.refs_0_, bf16[3072,1024]{1,0:T(8,128)(2,1)S(1)} %get-tuple-element.29.beside_ref.refs_1_, bf16[3072,1024]{1,0:T(8,128)(2,1)S(1)} %weight_load.1.beside_ref.refs_2_), custom_call_target="tpu_custom_call" | custom-call | flops 1207959552 | bytes 9437184 | tf_op jit(solution)/shard_map/near/pallas_call | solution.py:34
  28.2 0.3 %collective-permute-done.9.refs_4_ = bf16[128,1664]{1,0:T(8,128)(2,1)S(1)} collective-permute-done((bf16[128,1664]{1,0:T(8,128)(2,1)S(1)}, bf16[128,1664]{1,0:T(8,128)(2,1)S(1)}, u32[]{:S(2)}, u32[]{:S(2)}) %collective-permute-start.9) | collective-permute-done | bytes 426016 | tf_op jit(solution)/shard_map/ppermute | solution.py:420
  28.6 2.1 %far.1 = bf16[128,3072]{1,0:T(8,128)(2,1)} custom-call(f32[128,3072]{1,0:T(8,128)S(1)} %near.1.near_ref, bf16[3072,1024]{1,0:T(8,128)(2,1)S(1)} %get-tuple-element.34.refs_0_, bf16[3072,1024]{1,0:T(8,128)(2,1)S(1)} %get-tuple-element.29.beside_ref.refs_1_, bf16[3072,1024]{1,0:T(8,128)(2,1)S(1)} %weight_load.1.beside_ref.refs_2_, ...), custom_call_target="tpu_custom_call" | custom-call | flops 1207959552 | bytes 9437184 | tf_op jit(solution)/shard_map/far/pallas_call | solution.py:34
Async XLA Ops:
  2.2 7.7 %collective-permute-start = (bf16[304,128]{1,0:T(8,128)(2,1)S(1)}, bf16[304,128]{1,0:T(8,128)(2,1)S(1)}, u32[]{:S(2)}, u32[]{:S(2)}) collective-permute-start(bf16[304,128]{1,0:T(8,128)(2,1)S(1)} %get-tuple-element.25), channel_id=1, source_target_pairs={{0,6},{1,7},{2,4},{3,5},{4,2},{5,3},{6,0},{7,1},{8,14},{9,15},{10,... | collective-permute-start | bytes 233480 | tf_op jit(solution)/shard_map/ppermute | solution.py:342
  6.2 4.6 %collective-permute-start.1 = (bf16[304,128]{1,0:T(8,128)(2,1)S(1)}, bf16[304,128]{1,0:T(8,128)(2,1)S(1)}, u32[]{:S(2)}, u32[]{:S(2)}) collective-permute-start(bf16[304,128]{1,0:T(8,128)(2,1)S(1)} %get-tuple-element.26), channel_id=1, source_target_pairs={{0,2},{1,5},{2,0},{3,7},{4,6},{5,1},{6,4},{7,3},{8,10},{9,13},{10,... | collective-permute-start | bytes 233480 | tf_op jit(solution)/shard_map/ppermute | solution.py:342
  6.7 4.4 %collective-permute-start.2 = (bf16[304,128]{1,0:T(8,128)(2,1)S(1)}, bf16[304,128]{1,0:T(8,128)(2,1)S(1)}, u32[]{:S(2)}, u32[]{:S(2)}) collective-permute-start(bf16[304,128]{1,0:T(8,128)(2,1)S(1)} %get-tuple-element.27), channel_id=1, source_target_pairs={{0,4},{1,3},{2,6},{3,1},{4,0},{5,7},{6,2},{7,5},{8,12},{9,11},{10,... | collective-permute-start | bytes 233480 | tf_op jit(solution)/shard_map/ppermute | solution.py:342
  11.2 7.9 %collective-permute-start.5 = (bf16[304,128]{1,0:T(8,128)(2,1)S(1)}, bf16[304,128]{1,0:T(8,128)(2,1)S(1)}, u32[]{:S(2)}, u32[]{:S(2)}) collective-permute-start(bf16[304,128]{1,0:T(8,128)(2,1)S(1)} %group_state.1.after_ref), channel_id=1, source_target_pairs={{0,8},{1,9},{2,10},{3,11},{4,12},{5,13},{6,14},{7,15},{8,0},{9,1},... | collective-permute-start | bytes 233480 | tf_op jit(solution)/shard_map/ppermute | solution.py:342
  12.8 6.5 %collective-permute-start.4 = (bf16[304,128]{1,0:T(8,128)(2,1)S(1)}, bf16[304,128]{1,0:T(8,128)(2,1)S(1)}, u32[]{:S(2)}, u32[]{:S(2)}) collective-permute-start(bf16[304,128]{1,0:T(8,128)(2,1)S(1)} %group_state.1.after_ref), channel_id=1, source_target_pairs={{0,16},{1,17},{2,18},{3,19},{4,20},{5,21},{6,22},{7,23},{8,24},{9,... | collective-permute-start | bytes 233480 | tf_op jit(solution)/shard_map/ppermute | solution.py:342
  15.4 3.9 %collective-permute-start.3 = (bf16[304,128]{1,0:T(8,128)(2,1)S(1)}, bf16[304,128]{1,0:T(8,128)(2,1)S(1)}, u32[]{:S(2)}, u32[]{:S(2)}) collective-permute-start(bf16[304,128]{1,0:T(8,128)(2,1)S(1)} %group_state.1.after_ref), channel_id=1, source_target_pairs={{0,0},{1,1},{2,2},{3,3},{4,4},{5,5},{6,6},{7,7},{8,16},{9,17},{10,... | collective-permute-start | bytes 233480 | tf_op jit(solution)/shard_map/ppermute | solution.py:342
  19.5 6.4 %collective-permute-start.6 = (bf16[288,128]{1,0:T(8,128)(2,1)S(1)}, bf16[288,128]{1,0:T(8,128)(2,1)S(1)}, u32[]{:S(2)}, u32[]{:S(2)}) collective-permute-start(bf16[288,128]{1,0:T(8,128)(2,1)S(1)} %get-tuple-element.31), channel_id=1, source_target_pairs={{0,6},{1,7},{2,4},{3,5},{4,2},{5,3},{6,0},{7,1},{8,14},{9,15},{10,... | collective-permute-start | bytes 221192 | tf_op jit(solution)/shard_map/ppermute | solution.py:342
  21.3 4.6 %collective-permute-start.7 = (bf16[288,128]{1,0:T(8,128)(2,1)S(1)}, bf16[288,128]{1,0:T(8,128)(2,1)S(1)}, u32[]{:S(2)}, u32[]{:S(2)}) collective-permute-start(bf16[288,128]{1,0:T(8,128)(2,1)S(1)} %get-tuple-element.32), channel_id=1, source_target_pairs={{0,2},{1,5},{2,0},{3,7},{4,6},{5,1},{6,4},{7,3},{8,10},{9,13},{10,... | collective-permute-start | bytes 221192 | tf_op jit(solution)/shard_map/ppermute | solution.py:342
  21.8 4.4 %collective-permute-start.8 = (bf16[288,128]{1,0:T(8,128)(2,1)S(1)}, bf16[288,128]{1,0:T(8,128)(2,1)S(1)}, u32[]{:S(2)}, u32[]{:S(2)}) collective-permute-start(bf16[288,128]{1,0:T(8,128)(2,1)S(1)} %get-tuple-element.33), channel_id=1, source_target_pairs={{0,4},{1,3},{2,6},{3,1},{4,0},{5,7},{6,2},{7,5},{8,12},{9,11},{10,... | collective-permute-start | bytes 221192 | tf_op jit(solution)/shard_map/ppermute | solution.py:342
  26.7 1.8 %collective-permute-start.9 = (bf16[128,1664]{1,0:T(8,128)(2,1)S(1)}, bf16[128,1664]{1,0:T(8,128)(2,1)S(1)}, u32[]{:S(2)}, u32[]{:S(2)}) collective-permute-start(bf16[128,1664]{1,0:T(8,128)(2,1)S(1)} %hidden.1.hidden_ref.refs_3_), channel_id=1, source_target_pairs={{0,1},{1,0},{2,3},{3,2},{4,5},{5,4},{6,7},{7,6},{8,9},{9,8},{10,11... | collective-permute-start | bytes 1277960 | tf_op jit(solution)/shard_map/ppermute | solution.py:420

commit v5 on v4

--- a/solution.py
+++ b/solution.py
@@ -88,7 +88,7 @@
     pairs = [(doc_hbm, doc_ref)]
     for unit in helpers(group)[1]:
         cols = pl.ds(pl.multiple_of(unit * UC, LANES), UC)
-        columns.append(cols)
+        columns.append((unit, cols))
         pairs += [(key_hbm.at[:, cols], key_ref.at[:, cols])]
         pairs += [(value_hbm.at[:, cols], value_ref.at[:, cols])]
     copies = fetch(pairs, sems)
@@ -96,24 +96,24 @@
     ids = doc_ref[...].astype(f32)
     first = jnp.min(ids, axis=1, keepdims=True)
     last = jnp.max(ids, axis=1, keepdims=True)
-    keep = id_column(ids) == last
-    keep = jnp.concatenate([keep] * (UC // keep.shape[1]), axis=1)
-    head = lane_head((HD, UC))
+    keep = jnp.where(ids == last, 1.0, 0.0).astype(bf16)
+    lane = lax.broadcasted_iota(jnp.int32, (HD, LANES), 1)
     marks = jnp.where(
         lax.broadcasted_iota(jnp.int32, (IDS, LANES), 0) < IDS // 2,
         jnp.broadcast_to(last, (IDS, LANES)),
         jnp.broadcast_to(first, (IDS, LANES)),
     ).astype(bf16)
-    for i, cols in enumerate(columns):
+    for i, (unit, cols) in enumerate(columns):
         copies[2 * i + 1].wait()
         copies[2 * i + 2].wait()
-        keys = jnp.where(keep, key_ref[:, cols], jnp.zeros((), bf16))
-        full = lax.dot_general(
-            keys, value_ref[:, cols], (((0,), (0,)), ((), ())), preferred_element_type=f32
-        )
-        state = diagonal([full[a * HD : (a + 1) * HD] for a in range(UNIT)], head).astype(bf16)
+        turned = key_ref[:, cols].T * keep
         for c in range(UC // LANES):
-            packets[i][c * HD : (c + 1) * HD] = state[:, c * LANES : (c + 1) * LANES]
+            tile = pl.ds(pl.multiple_of(unit * UC + c * LANES, LANES), LANES)
+            full = jnp.dot(
+                turned[c * HD : (c + 2) * HD], value_ref[:, tile], preferred_element_type=f32
+            )
+            state = jnp.where(lane < HD - c * (LANES - HD), full[:HD], full[HD:])
+            packets[i][c * HD : (c + 1) * HD] = state.astype(bf16)
         packets[i][BODY:] = marks
 
 

time: 31 us -> 30.8 us (level)
  no operation moved by 1% of the time
where the time goes in v5:
time: 30.8 us; the launch traced here: 30.5 us
  Pallas kernels  15.3 us (50%)
  starting transfers between devices  13.1 us (43%)
  waiting for transfers between devices  1.92 us (6%)
    pallas_call x9, Pallas kernels, call(): pl.pallas_call(kernel, out_shape=outs, in_specs=[IN_HBM if i in far_in el...  15.3 us
    ppermute x9, starting transfers between devices, swap(): return lax.ppermute(value, ('seq', 'tp'), pairs)  13 us
    ppermute x9, waiting for transfers between devices, swap(): return lax.ppermute(value, ('seq', 'tp'), pairs)  1.59 us
  transfers between devices with their start and end apart: 10, of which 5 were waited for; matrix products, arithmetic and copies ran while one was open for 0% of the time, Pallas kernels for 34%

profile of v5, /device:TPU:0, one launch (start us, length us, event | category | flops | bytes accessed | tf_op | source)
XLA Modules:
  0.0 30.5 jit_solution(14664671579289895676)
XLA Ops:
  0.0 2.0 %own_states.1 = (bf16[304,128]{1,0:T(8,128)(2,1)S(1)}, bf16[304,128]{1,0:T(8,128)(2,1)S(1)}, bf16[304,128]{1,0:T(8,128)(2,1)S(1)}, bf16[304,128]{1,0:T(8,128)(2,...) custom-call(bf16[128,1536]{1,0:T(8,128)(2,1)} %key_hbm.1, bf16[128,1536]{1,0:T(8,128)(2,1)} %value_hbm.1, ...), custom_call_target="tpu_custom_call" | custom-call | tf_op jit(solution)/shard_map/own_states/pallas_call | solution.py:34
  2.0 4.0 %collective-permute-start = (bf16[304,128]{1,0:T(8,128)(2,1)S(1)}, bf16[304,128]{1,0:T(8,128)(2,1)S(1)}, u32[]{:S(2)}, u32[]{:S(2)}) collective-permute-start(bf16[304,128]{1,0:T(8,128)(2,1)S(1)} %get-tuple-element.25), channel_id=1, source_target_pairs={{0,6},{1,7},{2,4},{3,5},{4,2},{5,3},{6,0},{7,1},{8,14},{9,15},{10,... | collective-permute-start | bytes 233480 | tf_op jit(solution)/shard_map/ppermute | solution.py:342
  5.9 0.5 %collective-permute-start.1 = (bf16[304,128]{1,0:T(8,128)(2,1)S(1)}, bf16[304,128]{1,0:T(8,128)(2,1)S(1)}, u32[]{:S(2)}, u32[]{:S(2)}) collective-permute-start(bf16[304,128]{1,0:T(8,128)(2,1)S(1)} %get-tuple-element.26), channel_id=1, source_target_pairs={{0,2},{1,5},{2,0},{3,7},{4,6},{5,1},{6,4},{7,3},{8,10},{9,13},{10,... | collective-permute-start | bytes 233480 | tf_op jit(solution)/shard_map/ppermute | solution.py:342
  6.5 0.1 collective-permute-start.2
  6.6 3.1 %intra.1 = (f32[128,1536]{1,0:T(8,128)S(1)}, bf16[128,1536]{1,0:T(8,128)(2,1)S(1)}, bf16[3072,1024]{1,0:T(8,128)(2,1)S(1)}) custom-call(bf16[304,128]{1,0:T(8,128)(2,1)S(1)} %get-tuple-element.20.after_ref.refs_0_, bf16[128,1536]{1,0:T(8,128)(2,1)S(1)} %get-tuple-element.21.key_ref, bf16[128,1536]{1,0:T(8,128)(2,1)S(1)} %get-tuple-element.22.value_ref, ...), custom_call_target="tpu_custom_call" | custom-call | flops 402653184 | bytes 12582912 | tf_op jit(solution)/shard_map/intra/pallas_call | solution.py:34
  9.7 0.0 collective-permute-done.refs_1_
  9.7 0.8 %collective-permute-done.1.refs_2_ = bf16[304,128]{1,0:T(8,128)(2,1)S(1)} collective-permute-done((bf16[304,128]{1,0:T(8,128)(2,1)S(1)}, bf16[304,128]{1,0:T(8,128)(2,1)S(1)}, u32[]{:S(2)}, u32[]{:S(2)}) %collective-permute-start.1) | collective-permute-done | bytes 77856 | tf_op jit(solution)/shard_map/ppermute | solution.py:342
  10.5 0.4 %collective-permute-done.2.refs_3_ = bf16[304,128]{1,0:T(8,128)(2,1)S(1)} collective-permute-done((bf16[304,128]{1,0:T(8,128)(2,1)S(1)}, bf16[304,128]{1,0:T(8,128)(2,1)S(1)}, u32[]{:S(2)}, u32[]{:S(2)}) %collective-permute-start.2) | collective-permute-done | bytes 77856 | tf_op jit(solution)/shard_map/ppermute | solution.py:342
  10.9 0.1 group_state.1.after_ref
  10.9 1.6 %collective-permute-start.5 = (bf16[304,128]{1,0:T(8,128)(2,1)S(1)}, bf16[304,128]{1,0:T(8,128)(2,1)S(1)}, u32[]{:S(2)}, u32[]{:S(2)}) collective-permute-start(bf16[304,128]{1,0:T(8,128)(2,1)S(1)} %group_state.1.after_ref), channel_id=1, source_target_pairs={{0,8},{1,9},{2,10},{3,11},{4,12},{5,13},{6,14},{7,15},{8,0},{9,1},... | collective-permute-start | bytes 233480 | tf_op jit(solution)/shard_map/ppermute | solution.py:342
  12.6 2.6 %collective-permute-start.4 = (bf16[304,128]{1,0:T(8,128)(2,1)S(1)}, bf16[304,128]{1,0:T(8,128)(2,1)S(1)}, u32[]{:S(2)}, u32[]{:S(2)}) collective-permute-start(bf16[304,128]{1,0:T(8,128)(2,1)S(1)} %group_state.1.after_ref), channel_id=1, source_target_pairs={{0,16},{1,17},{2,18},{3,19},{4,20},{5,21},{6,22},{7,23},{8,24},{9,... | collective-permute-start | bytes 233480 | tf_op jit(solution)/shard_map/ppermute | solution.py:342
  15.2 0.7 %collective-permute-start.3 = (bf16[304,128]{1,0:T(8,128)(2,1)S(1)}, bf16[304,128]{1,0:T(8,128)(2,1)S(1)}, u32[]{:S(2)}, u32[]{:S(2)}) collective-permute-start(bf16[304,128]{1,0:T(8,128)(2,1)S(1)} %group_state.1.after_ref), channel_id=1, source_target_pairs={{0,0},{1,1},{2,2},{3,3},{4,4},{5,5},{6,6},{7,7},{8,16},{9,17},{10,... | collective-permute-start | bytes 233480 | tf_op jit(solution)/shard_map/ppermute | solution.py:342
  15.8 3.0 %gate.1 = (f32[128,1536]{1,0:T(8,128)S(1)}, bf16[3072,1024]{1,0:T(8,128)(2,1)S(1)}) custom-call(bf16[304,128]{1,0:T(8,128)(2,1)S(1)} %group_state.1.after_ref, bf16[128,1536]{1,0:T(8,128)(2,1)} %gate_hbm.1, f32[1,3072]{1,0:T(1,128)} %bitcast.2, bf16[3072,3072]{1,0:T(8,128)(2,1)} %weight_hbm.5), custom_call_target="tpu_custom_call" | custom-call | bytes 12582912 | tf_op jit(solution)/shard_map/gate/pallas_call | solution.py:34
  18.9 0.0 collective-permute-done.5.refs_6_
  18.9 0.2 collective-permute-done.4.refs_5_
  19.1 0.0 collective-permute-done.3.refs_4_
  19.1 0.2 prefix_states.1
  19.2 1.8 %collective-permute-start.6 = (bf16[288,128]{1,0:T(8,128)(2,1)S(1)}, bf16[288,128]{1,0:T(8,128)(2,1)S(1)}, u32[]{:S(2)}, u32[]{:S(2)}) collective-permute-start(bf16[288,128]{1,0:T(8,128)(2,1)S(1)} %get-tuple-element.31), channel_id=1, source_target_pairs={{0,6},{1,7},{2,4},{3,5},{4,2},{5,3},{6,0},{7,1},{8,14},{9,15},{10,... | collective-permute-start | bytes 221192 | tf_op jit(solution)/shard_map/ppermute | solution.py:342
  21.1 0.5 %collective-permute-start.7 = (bf16[288,128]{1,0:T(8,128)(2,1)S(1)}, bf16[288,128]{1,0:T(8,128)(2,1)S(1)}, u32[]{:S(2)}, u32[]{:S(2)}) collective-permute-start(bf16[288,128]{1,0:T(8,128)(2,1)S(1)} %get-tuple-element.32), channel_id=1, source_target_pairs={{0,2},{1,5},{2,0},{3,7},{4,6},{5,1},{6,4},{7,3},{8,10},{9,13},{10,... | collective-permute-start | bytes 221192 | tf_op jit(solution)/shard_map/ppermute | solution.py:342
  21.6 1.2 %collective-permute-start.8 = (bf16[288,128]{1,0:T(8,128)(2,1)S(1)}, bf16[288,128]{1,0:T(8,128)(2,1)S(1)}, u32[]{:S(2)}, u32[]{:S(2)}) collective-permute-start(bf16[288,128]{1,0:T(8,128)(2,1)S(1)} %get-tuple-element.33), channel_id=1, source_target_pairs={{0,4},{1,3},{2,6},{3,1},{4,0},{5,7},{6,2},{7,5},{8,12},{9,11},{10,... | collective-permute-start | bytes 221192 | tf_op jit(solution)/shard_map/ppermute | solution.py:342
  22.8 2.9 %weight_load.1.beside_ref.refs_2_ = bf16[3072,1024]{1,0:T(8,128)(2,1)S(1)} custom-call(bf16[288,128]{1,0:T(8,128)(2,1)S(1)} %get-tuple-element.30.after_ref.refs_0_, bf16[3072,3072]{1,0:T(8,128)(2,1)} %weight_hbm.5), custom_call_target="tpu_custom_call" | custom-call | bytes 12582912 | tf_op jit(solution)/shard_map/weight_load/pallas_call | solution.py:34
  25.7 0.0 collective-permute-done.6.refs_1_
  25.7 0.0 collective-permute-done.7.refs_2_
  25.7 0.2 collective-permute-done.8.refs_3_
  25.9 0.6 %hidden.1.hidden_ref.refs_3_ = bf16[128,1664]{1,0:T(8,128)(2,1)S(1)} custom-call(bf16[128,1536]{1,0:T(8,128)(2,1)S(1)} %get-tuple-element.23.open_ref, f32[128,1536]{1,0:T(8,128)S(1)} %get-tuple-element.24.beside_ref.intra_ref, f32[128,1536]{1,0:T(8,128)S(1)} %get-tuple-element.28.scale_ref, bf16[3072,1024]{1,0:T(8,128)(2,1)S(1)} %weight_load.1.beside_ref.refs_2_, ...), custom_call_target="tpu_custom_call" | custom-call | tf_op jit(solution)/shard_map/hidden/pallas_call | solution.py:34
  26.5 0.1 collective-permute-start.9
  26.6 1.4 %near.1.near_ref = f32[128,3072]{1,0:T(8,128)S(1)} custom-call(bf16[128,1664]{1,0:T(8,128)(2,1)S(1)} %hidden.1.hidden_ref.refs_3_, bf16[3072,1024]{1,0:T(8,128)(2,1)S(1)} %get-tuple-element.34.refs_0_, bf16[3072,1024]{1,0:T(8,128)(2,1)S(1)} %get-tuple-element.29.beside_ref.refs_1_, bf16[3072,1024]{1,0:T(8,128)(2,1)S(1)} %weight_load.1.beside_ref.refs_2_), custom_call_target="tpu_custom_call" | custom-call | flops 1207959552 | bytes 9437184 | tf_op jit(solution)/shard_map/near/pallas_call | solution.py:34
  28.0 0.3 %collective-permute-done.9.refs_4_ = bf16[128,1664]{1,0:T(8,128)(2,1)S(1)} collective-permute-done((bf16[128,1664]{1,0:T(8,128)(2,1)S(1)}, bf16[128,1664]{1,0:T(8,128)(2,1)S(1)}, u32[]{:S(2)}, u32[]{:S(2)}) %collective-permute-start.9) | collective-permute-done | bytes 426016 | tf_op jit(solution)/shard_map/ppermute | solution.py:420
  28.3 2.1 %far.1 = bf16[128,3072]{1,0:T(8,128)(2,1)} custom-call(f32[128,3072]{1,0:T(8,128)S(1)} %near.1.near_ref, bf16[3072,1024]{1,0:T(8,128)(2,1)S(1)} %get-tuple-element.34.refs_0_, bf16[3072,1024]{1,0:T(8,128)(2,1)S(1)} %get-tuple-element.29.beside_ref.refs_1_, bf16[3072,1024]{1,0:T(8,128)(2,1)S(1)} %weight_load.1.beside_ref.refs_2_, ...), custom_call_target="tpu_custom_call" | custom-call | flops 1207959552 | bytes 9437184 | tf_op jit(solution)/shard_map/far/pallas_call | solution.py:34
Async XLA Ops:
  2.0 7.7 %collective-permute-start = (bf16[304,128]{1,0:T(8,128)(2,1)S(1)}, bf16[304,128]{1,0:T(8,128)(2,1)S(1)}, u32[]{:S(2)}, u32[]{:S(2)}) collective-permute-start(bf16[304,128]{1,0:T(8,128)(2,1)S(1)} %get-tuple-element.25), channel_id=1, source_target_pairs={{0,6},{1,7},{2,4},{3,5},{4,2},{5,3},{6,0},{7,1},{8,14},{9,15},{10,... | collective-permute-start | bytes 233480 | tf_op jit(solution)/shard_map/ppermute | solution.py:342
  5.9 4.6 %collective-permute-start.1 = (bf16[304,128]{1,0:T(8,128)(2,1)S(1)}, bf16[304,128]{1,0:T(8,128)(2,1)S(1)}, u32[]{:S(2)}, u32[]{:S(2)}) collective-permute-start(bf16[304,128]{1,0:T(8,128)(2,1)S(1)} %get-tuple-element.26), channel_id=1, source_target_pairs={{0,2},{1,5},{2,0},{3,7},{4,6},{5,1},{6,4},{7,3},{8,10},{9,13},{10,... | collective-permute-start | bytes 233480 | tf_op jit(solution)/shard_map/ppermute | solution.py:342
  6.5 4.4 %collective-permute-start.2 = (bf16[304,128]{1,0:T(8,128)(2,1)S(1)}, bf16[304,128]{1,0:T(8,128)(2,1)S(1)}, u32[]{:S(2)}, u32[]{:S(2)}) collective-permute-start(bf16[304,128]{1,0:T(8,128)(2,1)S(1)} %get-tuple-element.27), channel_id=1, source_target_pairs={{0,4},{1,3},{2,6},{3,1},{4,0},{5,7},{6,2},{7,5},{8,12},{9,11},{10,... | collective-permute-start | bytes 233480 | tf_op jit(solution)/shard_map/ppermute | solution.py:342
  10.9 7.9 %collective-permute-start.5 = (bf16[304,128]{1,0:T(8,128)(2,1)S(1)}, bf16[304,128]{1,0:T(8,128)(2,1)S(1)}, u32[]{:S(2)}, u32[]{:S(2)}) collective-permute-start(bf16[304,128]{1,0:T(8,128)(2,1)S(1)} %group_state.1.after_ref), channel_id=1, source_target_pairs={{0,8},{1,9},{2,10},{3,11},{4,12},{5,13},{6,14},{7,15},{8,0},{9,1},... | collective-permute-start | bytes 233480 | tf_op jit(solution)/shard_map/ppermute | solution.py:342
  12.6 6.5 %collective-permute-start.4 = (bf16[304,128]{1,0:T(8,128)(2,1)S(1)}, bf16[304,128]{1,0:T(8,128)(2,1)S(1)}, u32[]{:S(2)}, u32[]{:S(2)}) collective-permute-start(bf16[304,128]{1,0:T(8,128)(2,1)S(1)} %group_state.1.after_ref), channel_id=1, source_target_pairs={{0,16},{1,17},{2,18},{3,19},{4,20},{5,21},{6,22},{7,23},{8,24},{9,... | collective-permute-start | bytes 233480 | tf_op jit(solution)/shard_map/ppermute | solution.py:342
  15.2 3.9 %collective-permute-start.3 = (bf16[304,128]{1,0:T(8,128)(2,1)S(1)}, bf16[304,128]{1,0:T(8,128)(2,1)S(1)}, u32[]{:S(2)}, u32[]{:S(2)}) collective-permute-start(bf16[304,128]{1,0:T(8,128)(2,1)S(1)} %group_state.1.after_ref), channel_id=1, source_target_pairs={{0,0},{1,1},{2,2},{3,3},{4,4},{5,5},{6,6},{7,7},{8,16},{9,17},{10,... | collective-permute-start | bytes 233480 | tf_op jit(solution)/shard_map/ppermute | solution.py:342
  19.2 6.4 %collective-permute-start.6 = (bf16[288,128]{1,0:T(8,128)(2,1)S(1)}, bf16[288,128]{1,0:T(8,128)(2,1)S(1)}, u32[]{:S(2)}, u32[]{:S(2)}) collective-permute-start(bf16[288,128]{1,0:T(8,128)(2,1)S(1)} %get-tuple-element.31), channel_id=1, source_target_pairs={{0,6},{1,7},{2,4},{3,5},{4,2},{5,3},{6,0},{7,1},{8,14},{9,15},{10,... | collective-permute-start | bytes 221192 | tf_op jit(solution)/shard_map/ppermute | solution.py:342
  21.1 4.6 %collective-permute-start.7 = (bf16[288,128]{1,0:T(8,128)(2,1)S(1)}, bf16[288,128]{1,0:T(8,128)(2,1)S(1)}, u32[]{:S(2)}, u32[]{:S(2)}) collective-permute-start(bf16[288,128]{1,0:T(8,128)(2,1)S(1)} %get-tuple-element.32), channel_id=1, source_target_pairs={{0,2},{1,5},{2,0},{3,7},{4,6},{5,1},{6,4},{7,3},{8,10},{9,13},{10,... | collective-permute-start | bytes 221192 | tf_op jit(solution)/shard_map/ppermute | solution.py:342
  21.6 4.4 %collective-permute-start.8 = (bf16[288,128]{1,0:T(8,128)(2,1)S(1)}, bf16[288,128]{1,0:T(8,128)(2,1)S(1)}, u32[]{:S(2)}, u32[]{:S(2)}) collective-permute-start(bf16[288,128]{1,0:T(8,128)(2,1)S(1)} %get-tuple-element.33), channel_id=1, source_target_pairs={{0,4},{1,3},{2,6},{3,1},{4,0},{5,7},{6,2},{7,5},{8,12},{9,11},{10,... | collective-permute-start | bytes 221192 | tf_op jit(solution)/shard_map/ppermute | solution.py:342
  26.5 1.8 %collective-permute-start.9 = (bf16[128,1664]{1,0:T(8,128)(2,1)S(1)}, bf16[128,1664]{1,0:T(8,128)(2,1)S(1)}, u32[]{:S(2)}, u32[]{:S(2)}) collective-permute-start(bf16[128,1664]{1,0:T(8,128)(2,1)S(1)} %hidden.1.hidden_ref.refs_3_), channel_id=1, source_target_pairs={{0,1},{1,0},{2,3},{3,2},{4,5},{5,4},{6,7},{7,6},{8,9},{9,8},{10,11... | collective-permute-start | bytes 1277960 | tf_op jit(solution)/shard_map/ppermute | solution.py:420

commit v6 on v5

--- a/solution.py
+++ b/solution.py
@@ -1,4 +1,5 @@
 import functools
+import math
 
 import jax
 import jax.numpy as jnp
@@ -17,7 +18,6 @@
 BODY = HD * (UC // LANES)
 IDS = 16
 PACKET = BODY + IDS
-LOADS = 4
 norm_eps = 1e-05
 
 bf16 = jnp.bfloat16
@@ -158,19 +158,24 @@
         out[...] = done[rows_of(place, BODY)]
 
 
-def start_load(weight_hbm, third, out_ref, sems):
-    rows, columns = out_ref.shape
-    step = rows // LOADS
-    return fetch(
-        [
-            (
-                weight_hbm.at[pl.ds(i * step, step), pl.ds(third * columns, columns)],
-                out_ref.at[pl.ds(i * step, step)],
-            )
-            for i in range(LOADS)
-        ],
-        sems,
-    )
+def chunks_of(depth, rows):
+    step = math.gcd(depth, rows // 3)
+    return step, [
+        (r // depth, r % depth, r // (rows // 3), r % (rows // 3)) for r in range(0, rows, step)
+    ]
+
+
+def start_load(weight_hbm, third, out_ref, sems, depth):
+    rows, parts = weight_hbm.shape[0], weight_hbm.shape[0] // depth
+    me = lax.axis_index("tp")
+    step, chunks = chunks_of(depth, rows)
+    pairs = []
+    for part, offset, piece, start in chunks:
+        if piece == third:
+            owner = lax.rem(me + parts - part, parts)
+            source = pl.ds(pl.multiple_of(owner * depth + offset, LANES), step)
+            pairs.append((weight_hbm.at[source], out_ref.at[pl.ds(start, step)]))
+    return fetch(pairs, sems)
 
 
 def gate_kernel(
@@ -179,8 +184,8 @@
     gate_ref, gain_ref, sems, load_sems,
 ):
     width = gate_ref.shape[1]
+    loads = start_load(weight_hbm, 1, weight_ref, load_sems, width)
     copies = fetch([(gate_hbm, gate_ref), (gain_hbm, gain_ref)], sems)
-    loads = start_load(weight_hbm, 1, weight_ref, load_sems)
     part = lax.axis_index("tp")
     for copy in copies:
         copy.wait()
@@ -192,8 +197,8 @@
         load.wait()
 
 
-def load_kernel(after_ref, weight_hbm, out_ref, sems):
-    for copy in start_load(weight_hbm, 2, out_ref, sems):
+def load_kernel(depth, after_ref, weight_hbm, out_ref, sems):
+    for copy in start_load(weight_hbm, 2, out_ref, sems, depth):
         copy.wait()
 
 
@@ -207,7 +212,7 @@
     copies = fetch(
         [(doc_hbm, doc_ref)] + [(query_hbm.at[:, c], query_ref.at[:, c]) for c in units], sems
     )
-    loads = start_load(weight_hbm, 0, weight_ref, load_sems)
+    loads = start_load(weight_hbm, 0, weight_ref, load_sems, width)
     copies[0].wait()
     ids = doc_ref[...].astype(f32)
     column = id_column(ids)
@@ -238,20 +243,14 @@
 
 
 def hidden_kernel(group, open_ref, intra_ref, scale_ref, beside_ref, *refs):
-    states, (out_ref, in_order) = refs[:group], refs[group:]
+    states, out_ref = refs[:group], refs[group]
     rows, width = open_ref.shape
-    for place, state in zip(helpers(group)[1], states):
-        in_order[rows_of(place, BODY)] = state[...]
     head = lane_head((HD, UC))
     squares = jnp.zeros((rows, LANES), f32)
-    for u in range(width // UC):
-        cols = slice(u * UC, (u + 1) * UC)
+    for unit, state_ref in zip(helpers(group)[1], states):
+        cols = pl.ds(pl.multiple_of(unit * UC, LANES), UC)
         state = jnp.concatenate(
-            [
-                in_order[u * BODY + c * HD : u * BODY + (c + 1) * HD]
-                for c in range(UC // LANES)
-            ],
-            axis=1,
+            [state_ref[c * HD : (c + 1) * HD] for c in range(UC // LANES)], axis=1
         )
         spread = jnp.concatenate(
             [jnp.where(head == a, state, jnp.zeros((), bf16)) for a in range(UNIT)], axis=0
@@ -269,22 +268,33 @@
     out_ref[:, width:] = jnp.where(lane < LANES // 2, high, low)
 
 
+def product(hidden, weights, cols, parts):
+    depth = hidden[0].shape[1] - LANES
+    step, chunks = chunks_of(depth, 3 * weights[0].shape[0])
+    total = None
+    for part, offset, piece, start in chunks:
+        if part in parts:
+            one = jnp.dot(
+                hidden[part][:, offset : offset + step],
+                weights[piece][start : start + step, cols],
+                preferred_element_type=f32,
+            )
+            total = one if total is None else total + one
+    return total
+
+
 def near_kernel(hidden_ref, *refs):
     *weights, out_ref = refs
-    depth = hidden_ref.shape[1] - LANES
-    rows = pl.ds(pl.multiple_of(lax.axis_index("tp") * depth, LANES), depth)
-    wide = weights[0].shape[1]
-    for i, weight in enumerate(weights):
-        out_ref[:, i * wide : (i + 1) * wide] = jnp.dot(
-            hidden_ref[:, :depth], weight[rows], preferred_element_type=f32
-        )
+    step = out_ref.shape[1] // 6
+    for i in range(6):
+        cols = pl.ds(i * step, step)
+        out_ref[:, cols] = product([hidden_ref], weights, cols, (0,))
 
 
 def far_kernel(parts, near_ref, *refs):
     weights, hidden, (out_hbm, out_ref, sems) = refs[:3], refs[3:-3], refs[-3:]
     depth = hidden[0].shape[1] - LANES
     step = out_ref.shape[1] // 6
-    me = lax.axis_index("tp")
     total = None
     for ref in hidden:
         one = ref[:, depth:].astype(f32)
@@ -293,16 +303,9 @@
     norm = lax.rsqrt(total / WIDTH + norm_eps)
     norm = jnp.concatenate([norm] * (step // LANES), axis=1)
     copies = []
-    pieces = [(w, c) for w in weights for c in range(0, w.shape[1], step)]
-    for i, (weight, column) in enumerate(pieces):
-        inner, cols = pl.ds(column, step), pl.ds(i * step, step)
-        value = near_ref[:, cols]
-        for k in range(1, parts):
-            owner = lax.rem(me + parts - k, parts)
-            rows = pl.ds(pl.multiple_of(owner * depth, LANES), depth)
-            value = value + jnp.dot(
-                hidden[k][:, :depth], weight[rows, inner], preferred_element_type=f32
-            )
+    for i in range(6):
+        cols = pl.ds(i * step, step)
+        value = near_ref[:, cols] + product(hidden, weights, cols, range(1, parts))
         out_ref[:, cols] = (value * norm).astype(bf16)
         copy = pltpu.make_async_copy(out_ref.at[:, cols], out_hbm.at[:, cols], sems.at[i])
         copy.start()
@@ -332,7 +335,8 @@
     body = jax.ShapeDtypeStruct((BODY, LANES), bf16)
     wide = jax.ShapeDtypeStruct((rows, width), f32)
     narrow = jax.ShapeDtypeStruct((rows, width), bf16)
-    third = pltpu.VMEM((out_weight.shape[0], features // 3), bf16)
+    third = pltpu.VMEM((out_weight.shape[0] // 3, features), bf16)
+    loads = out_weight.shape[0] // 3 // chunks_of(width, out_weight.shape[0])[0]
     moved = 4 * out_weight.size // 3
 
     def swap(value, partner):
@@ -369,7 +373,7 @@
         [wide, narrow, third],
         (own[0], key_block, value_block, queries, ids, out_weight),
         "intra",
-        scratch=[pltpu.VMEM((rows, width), bf16), ids_block, dma((1 + units,)), dma((LOADS,))],
+        scratch=[pltpu.VMEM((rows, width), bf16), ids_block, dma((1 + units,)), dma((loads,))],
         far_in=(3, 4, 5),
         flops=4 * rows * rows * UNIT * width,
         moved=moved,
@@ -387,7 +391,7 @@
             pltpu.VMEM((rows, width), bf16),
             pltpu.VMEM((1, WIDTH), f32),
             dma((2,)),
-            dma((LOADS,)),
+            dma((loads,)),
         ],
         far_in=(1, 2, 3),
         moved=moved,
@@ -401,11 +405,11 @@
     )
     states = trade(prefixes)
     (weight2,) = call(
-        load_kernel,
+        functools.partial(load_kernel, width),
         [third],
         (prefixes[0], out_weight),
         "weight_load",
-        scratch=[dma((LOADS,))],
+        scratch=[dma((loads,))],
         far_in=(1,),
         moved=moved,
     )
@@ -414,7 +418,6 @@
         [jax.ShapeDtypeStruct((rows, width + LANES), bf16)],
         (opened, intra, scale, weight2, *states),
         "hidden",
-        scratch=[pltpu.VMEM((group * BODY, LANES), bf16)],
     )
     others = [
         lax.ppermute(hidden, "tp", [(i, (i + k) % parts) for i in range(parts)])

time: 30.8 us -> 30.7 us (level)
  no operation moved by 1% of the time
where the time goes in v6:
time: 30.7 us; the launch traced here: 30.4 us
  Pallas kernels  15.3 us (50%)
  starting transfers between devices  13.1 us (43%)
  waiting for transfers between devices  1.92 us (6%)
    pallas_call x9, Pallas kernels, call(): pl.pallas_call(kernel, out_shape=outs, in_specs=[IN_HBM if i in far_in el...  15.3 us
    ppermute x9, starting transfers between devices, swap(): return lax.ppermute(value, ('seq', 'tp'), pairs)  13 us
    ppermute x9, waiting for transfers between devices, swap(): return lax.ppermute(value, ('seq', 'tp'), pairs)  1.57 us
  transfers between devices with their start and end apart: 10, of which 5 were waited for; matrix products, arithmetic and copies ran while one was open for 0% of the time, Pallas kernels for 34%

profile of v6, /device:TPU:0, one launch (start us, length us, event | category | flops | bytes accessed | tf_op | source)
XLA Modules:
  0.0 30.4 jit_solution(4692908494279068084)
XLA Ops:
  0.0 2.0 %own_states.1 = (bf16[304,128]{1,0:T(8,128)(2,1)S(1)}, bf16[304,128]{1,0:T(8,128)(2,1)S(1)}, bf16[304,128]{1,0:T(8,128)(2,1)S(1)}, bf16[304,128]{1,0:T(8,128)(2,...) custom-call(bf16[128,1536]{1,0:T(8,128)(2,1)} %key_hbm.1, bf16[128,1536]{1,0:T(8,128)(2,1)} %value_hbm.1, ...), custom_call_target="tpu_custom_call" | custom-call | tf_op jit(solution)/shard_map/own_states/pallas_call | solution.py:34
  2.0 4.0 %collective-permute-start = (bf16[304,128]{1,0:T(8,128)(2,1)S(1)}, bf16[304,128]{1,0:T(8,128)(2,1)S(1)}, u32[]{:S(2)}, u32[]{:S(2)}) collective-permute-start(bf16[304,128]{1,0:T(8,128)(2,1)S(1)} %get-tuple-element.25), channel_id=1, source_target_pairs={{0,6},{1,7},{2,4},{3,5},{4,2},{5,3},{6,0},{7,1},{8,14},{9,15},{10,... | collective-permute-start | bytes 233480 | tf_op jit(solution)/shard_map/ppermute | solution.py:346
  5.9 0.5 %collective-permute-start.1 = (bf16[304,128]{1,0:T(8,128)(2,1)S(1)}, bf16[304,128]{1,0:T(8,128)(2,1)S(1)}, u32[]{:S(2)}, u32[]{:S(2)}) collective-permute-start(bf16[304,128]{1,0:T(8,128)(2,1)S(1)} %get-tuple-element.26), channel_id=1, source_target_pairs={{0,2},{1,5},{2,0},{3,7},{4,6},{5,1},{6,4},{7,3},{8,10},{9,13},{10,... | collective-permute-start | bytes 233480 | tf_op jit(solution)/shard_map/ppermute | solution.py:346
  6.5 0.1 collective-permute-start.2
  6.6 3.1 %intra.1 = (f32[128,1536]{1,0:T(8,128)S(1)}, bf16[128,1536]{1,0:T(8,128)(2,1)S(1)}, bf16[1024,3072]{1,0:T(8,128)(2,1)S(1)}) custom-call(bf16[304,128]{1,0:T(8,128)(2,1)S(1)} %get-tuple-element.20.after_ref.refs_0_, bf16[128,1536]{1,0:T(8,128)(2,1)S(1)} %get-tuple-element.21.key_ref, bf16[128,1536]{1,0:T(8,128)(2,1)S(1)} %get-tuple-element.22.value_ref, ...), custom_call_target="tpu_custom_call" | custom-call | flops 402653184 | bytes 12582912 | tf_op jit(solution)/shard_map/intra/pallas_call | solution.py:34
  9.7 0.0 collective-permute-done.refs_1_
  9.7 0.8 %collective-permute-done.1.refs_2_ = bf16[304,128]{1,0:T(8,128)(2,1)S(1)} collective-permute-done((bf16[304,128]{1,0:T(8,128)(2,1)S(1)}, bf16[304,128]{1,0:T(8,128)(2,1)S(1)}, u32[]{:S(2)}, u32[]{:S(2)}) %collective-permute-start.1) | collective-permute-done | bytes 77856 | tf_op jit(solution)/shard_map/ppermute | solution.py:346
  10.5 0.4 %collective-permute-done.2.refs_3_ = bf16[304,128]{1,0:T(8,128)(2,1)S(1)} collective-permute-done((bf16[304,128]{1,0:T(8,128)(2,1)S(1)}, bf16[304,128]{1,0:T(8,128)(2,1)S(1)}, u32[]{:S(2)}, u32[]{:S(2)}) %collective-permute-start.2) | collective-permute-done | bytes 77856 | tf_op jit(solution)/shard_map/ppermute | solution.py:346
  10.9 0.1 group_state.1.after_ref
  10.9 1.6 %collective-permute-start.5 = (bf16[304,128]{1,0:T(8,128)(2,1)S(1)}, bf16[304,128]{1,0:T(8,128)(2,1)S(1)}, u32[]{:S(2)}, u32[]{:S(2)}) collective-permute-start(bf16[304,128]{1,0:T(8,128)(2,1)S(1)} %group_state.1.after_ref), channel_id=1, source_target_pairs={{0,8},{1,9},{2,10},{3,11},{4,12},{5,13},{6,14},{7,15},{8,0},{9,1},... | collective-permute-start | bytes 233480 | tf_op jit(solution)/shard_map/ppermute | solution.py:346
  12.6 2.6 %collective-permute-start.4 = (bf16[304,128]{1,0:T(8,128)(2,1)S(1)}, bf16[304,128]{1,0:T(8,128)(2,1)S(1)}, u32[]{:S(2)}, u32[]{:S(2)}) collective-permute-start(bf16[304,128]{1,0:T(8,128)(2,1)S(1)} %group_state.1.after_ref), channel_id=1, source_target_pairs={{0,16},{1,17},{2,18},{3,19},{4,20},{5,21},{6,22},{7,23},{8,24},{9,... | collective-permute-start | bytes 233480 | tf_op jit(solution)/shard_map/ppermute | solution.py:346
  15.2 0.7 %collective-permute-start.3 = (bf16[304,128]{1,0:T(8,128)(2,1)S(1)}, bf16[304,128]{1,0:T(8,128)(2,1)S(1)}, u32[]{:S(2)}, u32[]{:S(2)}) collective-permute-start(bf16[304,128]{1,0:T(8,128)(2,1)S(1)} %group_state.1.after_ref), channel_id=1, source_target_pairs={{0,0},{1,1},{2,2},{3,3},{4,4},{5,5},{6,6},{7,7},{8,16},{9,17},{10,... | collective-permute-start | bytes 233480 | tf_op jit(solution)/shard_map/ppermute | solution.py:346
  15.8 3.0 %gate.1 = (f32[128,1536]{1,0:T(8,128)S(1)}, bf16[1024,3072]{1,0:T(8,128)(2,1)S(1)}) custom-call(bf16[304,128]{1,0:T(8,128)(2,1)S(1)} %group_state.1.after_ref, bf16[128,1536]{1,0:T(8,128)(2,1)} %gate_hbm.1, f32[1,3072]{1,0:T(1,128)} %bitcast.2, bf16[3072,3072]{1,0:T(8,128)(2,1)} %weight_hbm.5), custom_call_target="tpu_custom_call" | custom-call | bytes 12582912 | tf_op jit(solution)/shard_map/gate/pallas_call | solution.py:34
  18.9 0.0 collective-permute-done.5.refs_6_
  18.9 0.2 collective-permute-done.4.refs_5_
  19.1 0.0 collective-permute-done.3.refs_4_
  19.1 0.2 prefix_states.1
  19.2 1.8 %collective-permute-start.6 = (bf16[288,128]{1,0:T(8,128)(2,1)S(1)}, bf16[288,128]{1,0:T(8,128)(2,1)S(1)}, u32[]{:S(2)}, u32[]{:S(2)}) collective-permute-start(bf16[288,128]{1,0:T(8,128)(2,1)S(1)} %get-tuple-element.31), channel_id=1, source_target_pairs={{0,6},{1,7},{2,4},{3,5},{4,2},{5,3},{6,0},{7,1},{8,14},{9,15},{10,... | collective-permute-start | bytes 221192 | tf_op jit(solution)/shard_map/ppermute | solution.py:346
  21.1 0.5 %collective-permute-start.7 = (bf16[288,128]{1,0:T(8,128)(2,1)S(1)}, bf16[288,128]{1,0:T(8,128)(2,1)S(1)}, u32[]{:S(2)}, u32[]{:S(2)}) collective-permute-start(bf16[288,128]{1,0:T(8,128)(2,1)S(1)} %get-tuple-element.32), channel_id=1, source_target_pairs={{0,2},{1,5},{2,0},{3,7},{4,6},{5,1},{6,4},{7,3},{8,10},{9,13},{10,... | collective-permute-start | bytes 221192 | tf_op jit(solution)/shard_map/ppermute | solution.py:346
  21.6 1.2 %collective-permute-start.8 = (bf16[288,128]{1,0:T(8,128)(2,1)S(1)}, bf16[288,128]{1,0:T(8,128)(2,1)S(1)}, u32[]{:S(2)}, u32[]{:S(2)}) collective-permute-start(bf16[288,128]{1,0:T(8,128)(2,1)S(1)} %get-tuple-element.33), channel_id=1, source_target_pairs={{0,4},{1,3},{2,6},{3,1},{4,0},{5,7},{6,2},{7,5},{8,12},{9,11},{10,... | collective-permute-start | bytes 221192 | tf_op jit(solution)/shard_map/ppermute | solution.py:346
  22.8 2.9 %weight_load.1.beside_ref.refs_2_ = bf16[1024,3072]{1,0:T(8,128)(2,1)S(1)} custom-call(bf16[288,128]{1,0:T(8,128)(2,1)S(1)} %get-tuple-element.30.after_ref.refs_0_, bf16[3072,3072]{1,0:T(8,128)(2,1)} %weight_hbm.5), custom_call_target="tpu_custom_call" | custom-call | bytes 12582912 | tf_op jit(solution)/shard_map/weight_load/pallas_call | solution.py:34
  25.7 0.0 collective-permute-done.6.refs_1_
  25.7 0.0 collective-permute-done.7.refs_2_
  25.7 0.3 collective-permute-done.8.refs_3_
  25.9 0.5 %hidden.1.hidden_ref.refs_3_ = bf16[128,1664]{1,0:T(8,128)(2,1)S(1)} custom-call(bf16[128,1536]{1,0:T(8,128)(2,1)S(1)} %get-tuple-element.23.open_ref, f32[128,1536]{1,0:T(8,128)S(1)} %get-tuple-element.24.beside_ref.intra_ref, f32[128,1536]{1,0:T(8,128)S(1)} %get-tuple-element.28.scale_ref, bf16[1024,3072]{1,0:T(8,128)(2,1)S(1)} %weight_load.1.beside_ref.refs_2_, ...), custom_call_target="tpu_custom_call" | custom-call | tf_op jit(solution)/shard_map/hidden/pallas_call | solution.py:34
  26.5 0.1 collective-permute-start.9
  26.6 1.4 %near.1.near_ref = f32[128,3072]{1,0:T(8,128)S(1)} custom-call(bf16[128,1664]{1,0:T(8,128)(2,1)S(1)} %hidden.1.hidden_ref.refs_3_, bf16[1024,3072]{1,0:T(8,128)(2,1)S(1)} %get-tuple-element.34.refs_0_, bf16[1024,3072]{1,0:T(8,128)(2,1)S(1)} %get-tuple-element.29.beside_ref.refs_1_, bf16[1024,3072]{1,0:T(8,128)(2,1)S(1)} %weight_load.1.beside_ref.refs_2_), custom_call_target="tpu_custom_call" | custom-call | flops 1207959552 | bytes 9437184 | tf_op jit(solution)/shard_map/near/pallas_call | solution.py:34
  28.0 0.4 %collective-permute-done.9.refs_4_ = bf16[128,1664]{1,0:T(8,128)(2,1)S(1)} collective-permute-done((bf16[128,1664]{1,0:T(8,128)(2,1)S(1)}, bf16[128,1664]{1,0:T(8,128)(2,1)S(1)}, u32[]{:S(2)}, u32[]{:S(2)}) %collective-permute-start.9) | collective-permute-done | bytes 426016 | tf_op jit(solution)/shard_map/ppermute | solution.py:423
  28.3 2.1 %far.1 = bf16[128,3072]{1,0:T(8,128)(2,1)} custom-call(f32[128,3072]{1,0:T(8,128)S(1)} %near.1.near_ref, bf16[1024,3072]{1,0:T(8,128)(2,1)S(1)} %get-tuple-element.34.refs_0_, bf16[1024,3072]{1,0:T(8,128)(2,1)S(1)} %get-tuple-element.29.beside_ref.refs_1_, bf16[1024,3072]{1,0:T(8,128)(2,1)S(1)} %weight_load.1.beside_ref.refs_2_, ...), custom_call_target="tpu_custom_call" | custom-call | flops 1207959552 | bytes 9437184 | tf_op jit(solution)/shard_map/far/pallas_call | solution.py:34
Async XLA Ops:
  2.0 7.8 %collective-permute-start = (bf16[304,128]{1,0:T(8,128)(2,1)S(1)}, bf16[304,128]{1,0:T(8,128)(2,1)S(1)}, u32[]{:S(2)}, u32[]{:S(2)}) collective-permute-start(bf16[304,128]{1,0:T(8,128)(2,1)S(1)} %get-tuple-element.25), channel_id=1, source_target_pairs={{0,6},{1,7},{2,4},{3,5},{4,2},{5,3},{6,0},{7,1},{8,14},{9,15},{10,... | collective-permute-start | bytes 233480 | tf_op jit(solution)/shard_map/ppermute | solution.py:346
  5.9 4.6 %collective-permute-start.1 = (bf16[304,128]{1,0:T(8,128)(2,1)S(1)}, bf16[304,128]{1,0:T(8,128)(2,1)S(1)}, u32[]{:S(2)}, u32[]{:S(2)}) collective-permute-start(bf16[304,128]{1,0:T(8,128)(2,1)S(1)} %get-tuple-element.26), channel_id=1, source_target_pairs={{0,2},{1,5},{2,0},{3,7},{4,6},{5,1},{6,4},{7,3},{8,10},{9,13},{10,... | collective-permute-start | bytes 233480 | tf_op jit(solution)/shard_map/ppermute | solution.py:346
  6.5 4.4 %collective-permute-start.2 = (bf16[304,128]{1,0:T(8,128)(2,1)S(1)}, bf16[304,128]{1,0:T(8,128)(2,1)S(1)}, u32[]{:S(2)}, u32[]{:S(2)}) collective-permute-start(bf16[304,128]{1,0:T(8,128)(2,1)S(1)} %get-tuple-element.27), channel_id=1, source_target_pairs={{0,4},{1,3},{2,6},{3,1},{4,0},{5,7},{6,2},{7,5},{8,12},{9,11},{10,... | collective-permute-start | bytes 233480 | tf_op jit(solution)/shard_map/ppermute | solution.py:346
  10.9 7.9 %collective-permute-start.5 = (bf16[304,128]{1,0:T(8,128)(2,1)S(1)}, bf16[304,128]{1,0:T(8,128)(2,1)S(1)}, u32[]{:S(2)}, u32[]{:S(2)}) collective-permute-start(bf16[304,128]{1,0:T(8,128)(2,1)S(1)} %group_state.1.after_ref), channel_id=1, source_target_pairs={{0,8},{1,9},{2,10},{3,11},{4,12},{5,13},{6,14},{7,15},{8,0},{9,1},... | collective-permute-start | bytes 233480 | tf_op jit(solution)/shard_map/ppermute | solution.py:346
  12.6 6.5 %collective-permute-start.4 = (bf16[304,128]{1,0:T(8,128)(2,1)S(1)}, bf16[304,128]{1,0:T(8,128)(2,1)S(1)}, u32[]{:S(2)}, u32[]{:S(2)}) collective-permute-start(bf16[304,128]{1,0:T(8,128)(2,1)S(1)} %group_state.1.after_ref), channel_id=1, source_target_pairs={{0,16},{1,17},{2,18},{3,19},{4,20},{5,21},{6,22},{7,23},{8,24},{9,... | collective-permute-start | bytes 233480 | tf_op jit(solution)/shard_map/ppermute | solution.py:346
  15.2 3.9 %collective-permute-start.3 = (bf16[304,128]{1,0:T(8,128)(2,1)S(1)}, bf16[304,128]{1,0:T(8,128)(2,1)S(1)}, u32[]{:S(2)}, u32[]{:S(2)}) collective-permute-start(bf16[304,128]{1,0:T(8,128)(2,1)S(1)} %group_state.1.after_ref), channel_id=1, source_target_pairs={{0,0},{1,1},{2,2},{3,3},{4,4},{5,5},{6,6},{7,7},{8,16},{9,17},{10,... | collective-permute-start | bytes 233480 | tf_op jit(solution)/shard_map/ppermute | solution.py:346
  19.2 6.4 %collective-permute-start.6 = (bf16[288,128]{1,0:T(8,128)(2,1)S(1)}, bf16[288,128]{1,0:T(8,128)(2,1)S(1)}, u32[]{:S(2)}, u32[]{:S(2)}) collective-permute-start(bf16[288,128]{1,0:T(8,128)(2,1)S(1)} %get-tuple-element.31), channel_id=1, source_target_pairs={{0,6},{1,7},{2,4},{3,5},{4,2},{5,3},{6,0},{7,1},{8,14},{9,15},{10,... | collective-permute-start | bytes 221192 | tf_op jit(solution)/shard_map/ppermute | solution.py:346
  21.1 4.6 %collective-permute-start.7 = (bf16[288,128]{1,0:T(8,128)(2,1)S(1)}, bf16[288,128]{1,0:T(8,128)(2,1)S(1)}, u32[]{:S(2)}, u32[]{:S(2)}) collective-permute-start(bf16[288,128]{1,0:T(8,128)(2,1)S(1)} %get-tuple-element.32), channel_id=1, source_target_pairs={{0,2},{1,5},{2,0},{3,7},{4,6},{5,1},{6,4},{7,3},{8,10},{9,13},{10,... | collective-permute-start | bytes 221192 | tf_op jit(solution)/shard_map/ppermute | solution.py:346
  21.6 4.4 %collective-permute-start.8 = (bf16[288,128]{1,0:T(8,128)(2,1)S(1)}, bf16[288,128]{1,0:T(8,128)(2,1)S(1)}, u32[]{:S(2)}, u32[]{:S(2)}) collective-permute-start(bf16[288,128]{1,0:T(8,128)(2,1)S(1)} %get-tuple-element.33), channel_id=1, source_target_pairs={{0,4},{1,3},{2,6},{3,1},{4,0},{5,7},{6,2},{7,5},{8,12},{9,11},{10,... | collective-permute-start | bytes 221192 | tf_op jit(solution)/shard_map/ppermute | solution.py:346
  26.5 1.8 %collective-permute-start.9 = (bf16[128,1664]{1,0:T(8,128)(2,1)S(1)}, bf16[128,1664]{1,0:T(8,128)(2,1)S(1)}, u32[]{:S(2)}, u32[]{:S(2)}) collective-permute-start(bf16[128,1664]{1,0:T(8,128)(2,1)S(1)} %hidden.1.hidden_ref.refs_3_), channel_id=1, source_target_pairs={{0,1},{1,0},{2,3},{3,2},{4,5},{5,4},{6,7},{7,6},{8,9},{9,8},{10,11... | collective-permute-start | bytes 1277960 | tf_op jit(solution)/shard_map/ppermute | solution.py:423
